TPU v7x, 32 devices: a whole 2x2x4 slice. The times are simulated.
32 devices in a mesh: section: 4 (over x, core), dp: 8 (over z, y).
Axes of the slice: x: 2, y: 2, z: 4, core: 2. Of those that a mesh axis runs over, the one named last changes fastest.
Arguments:
- patches: bfloat16 [32, 352, 768], P('dp'), may hold values from -6 to 6
- cotangent: bfloat16 [32, 352, 768], P('dp'), may hold values from -6 to 6
- mask_flags: int32 [32, 352], P('dp'), may hold values 0 or 1
- segments: int32 [32, 352], P('dp'), may hold values from 0 to 2, as said below
- mask_token: bfloat16 [768], replicated, may hold values from -6 to 6
- norm_gains: bfloat16 [4, 768], P('section'), may hold values from 0.5 to 1.5
- norm_shifts: bfloat16 [4, 768], P('section'), may hold values from -1.75 to 1.75
- w_first: bfloat16 [4, 768, 3072], P('section'), may hold values from -0.21875 to 0.21875
- first_bias: bfloat16 [4, 3072], P('section'), may hold values from -1.25 to 1.25
- down_half: bfloat16 [4, 1536, 768], P('section'), may hold values from -0.109375 to 0.109375
Outputs:
- boundaries: bfloat16 [4, 32, 352, 768], P('section', 'dp')
- boundary_grads: float32 [4, 32, 352, 768], P('section', 'dp')
- token_grad: float32 [768], replicated
- gain_grads: float32 [4, 768], P('section')
- shift_grads: float32 [4, 768], P('section')
- first_grads: float32 [4, 768, 3072], P('section')
- bias_grads: float32 [4, 3072], P('section')
- half_grads: float32 [4, 1536, 768], P('section')
Inputs may be any that keep to these rules, and one draw needn't show every extreme that they name: `segments`: each row holds two or three whole images numbered 0, 1, 2 from its start, each of 64 to 256 patches.
All inputs are finite; a program needn't handle non-finite values. No bound on the sum of `mask_flags` on one device may be relied on, other than what follows from the above.
Results may differ from a plain program's by a relative error of at most 0.015.
Values may be sent and summed in bfloat16 or wider, within the bound.
No kernel may reach another device: no remote copies, remote signals or barrier semaphores. Data moves between devices by JAX's collectives and lax.ppermute only.
A program may use at most 192 MiB of HBM per device.

v0:
```python
from functools import partial

import jax
import jax.numpy as jnp
from jax import lax
from jax.sharding import PartitionSpec as P

HEADS = 12


EPSILON = 1e-06
NEGATIVE = -1000000000.0


def from_behind(value, axis, steps):
    count = lax.axis_size(axis)
    initial, last = (max(0, -steps), min(count, count - steps))
    return lax.ppermute(value, axis, [(source, source + steps) for source in range(initial, last)])


def product(matrix_a, matrix_b):
    return jnp.dot(matrix_a, matrix_b, preferred_element_type=jnp.float32)


def product_left(matrix_a, matrix_b):
    return lax.dot_general(
        matrix_a, matrix_b, (((0,), (0,)), ((), ())), preferred_element_type=jnp.float32
    )


def product_right(matrix_a, matrix_b):
    return lax.dot_general(
        matrix_a, matrix_b, (((1,), (1,)), ((), ())), preferred_element_type=jnp.float32
    )


def layer_norm(current, gain_row, shift_row):
    average = jnp.mean(current, -1, keepdims=True)
    centred = current - average
    spread = jnp.mean(centred * centred, -1, keepdims=True)
    return centred * lax.rsqrt(spread + EPSILON) * gain_row + shift_row


def split_heads(matrix):
    return matrix.reshape(matrix.shape[0], HEADS, matrix.shape[1] // HEADS)


def join_heads(tensor):
    return tensor.reshape(tensor.shape[0], tensor.shape[1] * tensor.shape[2])


def project_inputs(normed_low, first_block, bias_row):
    model_width = normed_low.shape[1]
    projected = product(normed_low, first_block[:, : 3 * model_width])
    queries = (projected[:, :model_width] + bias_row[:model_width]).astype(jnp.bfloat16)
    key_rows = projected[:, model_width : 2 * model_width].astype(jnp.bfloat16)
    values = (
        projected[:, 2 * model_width : 3 * model_width] + bias_row[model_width : 2 * model_width]
    ).astype(jnp.bfloat16)
    return (queries, key_rows, values)


def attention_weights(queries, key_rows, segment_ids):
    score_scale = (queries.shape[1] // HEADS) ** (-0.5)
    scores = (
        jnp.einsum(
            "qhd,khd->hqk",
            split_heads(queries),
            split_heads(key_rows),
            preferred_element_type=jnp.float32,
        )
        * score_scale
    )
    same_image = segment_ids[:, None] == segment_ids[None, :]
    scores = jnp.where(same_image[None], scores, NEGATIVE)
    row_max = jnp.max(scores, -1, keepdims=True)
    raised = jnp.exp(scores - row_max)
    return raised / jnp.sum(raised, -1, keepdims=True)


def mix_values(weights_low, values):
    mixed = jnp.einsum(
        "hqk,khd->qhd", weights_low, split_heads(values), preferred_element_type=jnp.float32
    )
    return join_heads(mixed).astype(jnp.bfloat16)


def attention_forward(
    current, gain_row, shift_row, first_block, bias_row, down_block, down_bias, segment_ids
):
    model_width = current.shape[1]
    normed_low = layer_norm(current, gain_row, shift_row).astype(jnp.bfloat16)
    queries, key_rows, values = project_inputs(normed_low, first_block, bias_row)
    weights_soft = attention_weights(queries, key_rows, segment_ids)
    context = mix_values(weights_soft.astype(jnp.bfloat16), values)
    return (
        current
        + product(context, first_block[:, 3 * model_width :])
        + bias_row[2 * model_width : 3 * model_width]
    )


def mlp_forward(
    current, gain_row, shift_row, first_block, bias_row, down_block, down_bias, segment_ids
):
    normed_low = layer_norm(current, gain_row, shift_row).astype(jnp.bfloat16)
    hidden = product(normed_low, first_block) + bias_row
    active = jax.nn.gelu(hidden, approximate=False).astype(jnp.bfloat16)
    return current + product(active, down_block) + down_bias


def attention_backward(
    current,
    grad_out,
    gain_row,
    shift_row,
    first_block,
    bias_row,
    down_block,
    down_bias,
    segment_ids,
):
    model_width = current.shape[1]
    normed, norm_pullback = jax.vjp(layer_norm, current, gain_row, shift_row)
    normed_low = normed.astype(jnp.bfloat16)
    queries, key_rows, values = project_inputs(normed_low, first_block, bias_row)
    weights_soft = attention_weights(queries, key_rows, segment_ids)
    weights_low = weights_soft.astype(jnp.bfloat16)
    context = mix_values(weights_low, values)
    grad_float = grad_out.astype(jnp.float32)
    grad_output_proj = product_left(context, grad_out)
    grad_context = product_right(grad_out, first_block[:, 3 * model_width :]).astype(jnp.bfloat16)
    grad_weights = jnp.einsum(
        "qhd,khd->hqk",
        split_heads(grad_context),
        split_heads(values),
        preferred_element_type=jnp.float32,
    )
    grad_scores = (
        weights_soft * (grad_weights - jnp.sum(weights_soft * grad_weights, -1, keepdims=True))
    ).astype(jnp.bfloat16)
    score_scale = (model_width // HEADS) ** (-0.5)
    grad_queries = (
        join_heads(
            jnp.einsum(
                "hqk,khd->qhd",
                grad_scores,
                split_heads(key_rows),
                preferred_element_type=jnp.float32,
            )
        )
        * score_scale
    ).astype(jnp.bfloat16)
    grad_keys = (
        join_heads(
            jnp.einsum(
                "hqk,qhd->khd",
                grad_scores,
                split_heads(queries),
                preferred_element_type=jnp.float32,
            )
        )
        * score_scale
    ).astype(jnp.bfloat16)
    grad_values = join_heads(
        jnp.einsum(
            "hqk,qhd->khd",
            weights_low,
            split_heads(grad_context),
            preferred_element_type=jnp.float32,
        )
    ).astype(jnp.bfloat16)
    grad_projected = jnp.concatenate([grad_queries, grad_keys, grad_values], 1)
    grad_input_proj = product_left(normed_low, grad_projected)
    grad_normed = product_right(grad_projected, first_block[:, : 3 * model_width])
    grad_current, grad_gain, grad_shift = norm_pullback(grad_normed)
    grad_bias = jnp.concatenate(
        [
            jnp.sum(grad_queries.astype(jnp.float32), 0),
            jnp.sum(grad_values.astype(jnp.float32), 0),
            jnp.sum(grad_float, 0),
            jnp.zeros((model_width,), jnp.float32),
        ]
    )
    zero_half = jnp.zeros((2 * model_width, model_width), jnp.float32)
    grad_first = jnp.concatenate([grad_input_proj, grad_output_proj], 1)
    return (
        grad_current + grad_float,
        grad_gain,
        grad_shift,
        grad_first,
        grad_bias,
        zero_half,
        zero_half,
        jnp.zeros((model_width,), jnp.float32),
    )


def mlp_backward(
    current,
    grad_out,
    gain_row,
    shift_row,
    first_block,
    bias_row,
    down_block,
    down_bias,
    segment_ids,
):
    model_width = current.shape[1]
    normed, norm_pullback = jax.vjp(layer_norm, current, gain_row, shift_row)
    normed_low = normed.astype(jnp.bfloat16)
    hidden = product(normed_low, first_block) + bias_row
    active, gelu_pullback = jax.vjp(partial(jax.nn.gelu, approximate=False), hidden)
    active_low = active.astype(jnp.bfloat16)
    grad_float = grad_out.astype(jnp.float32)
    grad_down = product_left(active_low, grad_out)
    grad_active = product_right(grad_out, down_block)
    grad_hidden = gelu_pullback(grad_active)[0].astype(jnp.bfloat16)
    grad_up = product_left(normed_low, grad_hidden)
    grad_normed = product_right(grad_hidden, first_block)
    grad_current, grad_gain, grad_shift = norm_pullback(grad_normed)
    return (
        grad_current + grad_float,
        grad_gain,
        grad_shift,
        grad_up,
        jnp.sum(grad_hidden.astype(jnp.float32), 0),
        grad_down[2 * model_width :],
        grad_down[: 2 * model_width],
        jnp.sum(grad_float, 0),
    )


def shards(
    patches,
    cotangent,
    mask_flags,
    segments,
    mask_token,
    norm_gains,
    norm_shifts,
    w_first,
    first_bias,
    down_half,
):
    section_count = lax.axis_size("section")
    section_index = lax.axis_index("section")
    odd_section = section_index % 2 == 1
    micro_count, row_length, model_width = patches.shape
    hidden_width = w_first.shape[2]
    gain_row = norm_gains[0].astype(jnp.float32)
    shift_row = norm_shifts[0].astype(jnp.float32)
    first_block = w_first[0]
    bias_row = first_bias[0]
    own_half = down_half[0]
    prior_half, prior_tail = from_behind((own_half, bias_row[3 * model_width :]), "section", 1)
    down_block = jnp.concatenate([prior_half, own_half], 0)
    weights_all = (gain_row, shift_row, first_block, bias_row, down_block, prior_tail)
    starts = jnp.where(mask_flags[..., None] == 1, mask_token, patches)

    def run_forward(entry_rows, segment_ids):
        return lax.cond(
            odd_section,
            mlp_forward,
            attention_forward,
            entry_rows.astype(jnp.float32),
            *weights_all,
            segment_ids
        )

    def skip_forward(entry_rows, segment_ids):
        return jnp.zeros(entry_rows.shape, jnp.float32)

    def forward_step(counter, carry):
        incoming, saved_inputs, finals = carry
        micro_index = counter - section_index
        is_valid = (micro_index >= 0) & (micro_index < micro_count)
        slot_index = jnp.clip(micro_index, 0, micro_count - 1)
        entry_rows = jnp.where(section_index == 0, starts[slot_index], incoming)
        result = lax.cond(is_valid, run_forward, skip_forward, entry_rows, segments[slot_index])
        result_low = result.astype(jnp.bfloat16)
        saved_inputs = saved_inputs.at[slot_index].set(
            jnp.where(is_valid, entry_rows, saved_inputs[slot_index])
        )
        finals = finals.at[slot_index].set(jnp.where(is_valid, result_low, finals[slot_index]))
        incoming = from_behind(result_low, "section", 1)
        return (incoming, saved_inputs, finals)

    row_zeros = jnp.zeros((row_length, model_width), jnp.bfloat16)
    block_zeros = jnp.zeros((micro_count, row_length, model_width), jnp.bfloat16)
    _, saved_inputs, finals = lax.fori_loop(
        0, micro_count + section_count - 1, forward_step, (row_zeros, block_zeros, block_zeros)
    )
    zero_totals = (
        jnp.zeros((model_width,), jnp.float32),
        jnp.zeros((model_width,), jnp.float32),
        jnp.zeros((model_width, hidden_width), jnp.float32),
        jnp.zeros((hidden_width,), jnp.float32),
        jnp.zeros((2 * model_width, model_width), jnp.float32),
        jnp.zeros((2 * model_width, model_width), jnp.float32),
        jnp.zeros((model_width,), jnp.float32),
    )

    def run_backward(entry_rows, grad_rows, segment_ids):
        return lax.cond(
            odd_section,
            mlp_backward,
            attention_backward,
            entry_rows.astype(jnp.float32),
            grad_rows,
            *weights_all,
            segment_ids
        )

    def skip_backward(entry_rows, grad_rows, segment_ids):
        return (jnp.zeros((row_length, model_width), jnp.float32),) + zero_totals

    last_section = section_count - 1

    def backward_step(counter, carry):
        incoming, totals, back_rows, token_total = carry
        micro_index = micro_count - 1 - (counter - (last_section - section_index))
        is_valid = (micro_index >= 0) & (micro_index < micro_count)
        slot_index = jnp.clip(micro_index, 0, micro_count - 1)
        grad_rows = jnp.where(section_index == last_section, cotangent[slot_index], incoming)
        results = lax.cond(
            is_valid,
            run_backward,
            skip_backward,
            saved_inputs[slot_index],
            grad_rows,
            segments[slot_index],
        )
        grad_current = results[0]
        totals = tuple((running + addend for running, addend in zip(totals, results[1:])))
        sent_low = grad_current.astype(jnp.bfloat16)
        masked_here = mask_flags[slot_index][:, None] == 1
        first_section = section_index == 0
        kept_rows = jnp.where(
            first_section, jnp.where(masked_here, 0.0, grad_current), sent_low.astype(jnp.float32)
        )
        back_rows = back_rows.at[slot_index].set(
            jnp.where(is_valid, kept_rows, back_rows[slot_index])
        )
        token_part = jnp.sum(jnp.where(masked_here, grad_current, 0.0), 0)
        token_total = token_total + jnp.where(first_section & is_valid, token_part, 0.0)
        incoming = from_behind(sent_low, "section", -1)
        return (incoming, totals, back_rows, token_total)

    back_init = jnp.zeros((micro_count, row_length, model_width), jnp.float32)
    token_init = jnp.zeros((model_width,), jnp.float32)
    _, totals, back_rows, token_total = lax.fori_loop(
        0,
        micro_count + section_count - 1,
        backward_step,
        (row_zeros, zero_totals, back_init, token_init),
    )
    grad_gain, grad_shift, grad_first, grad_bias, half_own, half_out, tail_out = totals
    tail_pad = jnp.zeros((3 * model_width,), jnp.float32)
    back_half = from_behind(half_out.astype(jnp.bfloat16), "section", -1).astype(half_out.dtype)
    back_tail = from_behind(tail_out.astype(jnp.bfloat16), "section", -1).astype(tail_out.dtype)
    grad_half = half_own + back_half
    grad_bias = grad_bias + jnp.concatenate([tail_pad, back_tail])
    grad_gain, grad_shift, grad_first, grad_bias, grad_half = lax.psum(
        (grad_gain, grad_shift, grad_first, grad_bias, grad_half), "dp"
    )
    token_grad = lax.psum(token_total, ("section", "dp"))
    return (
        finals[None],
        back_rows[None],
        token_grad,
        grad_gain[None],
        grad_shift[None],
        grad_first[None],
        grad_bias[None],
        grad_half[None],
    )


def solution(mesh):
    return jax.shard_map(
        shards,
        mesh=mesh,
        in_specs=(
            P("dp", None, None),
            P("dp", None, None),
            P("dp", None),
            P("dp", None),
            P(),
            P("section", None),
            P("section", None),
            P("section", None, None),
            P("section", None),
            P("section", None, None),
        ),
        out_specs=(
            P("section", "dp", None, None),
            P("section", "dp", None, None),
            P(),
            P("section", None),
            P("section", None),
            P("section", None, None),
            P("section", None),
            P("section", None, None),
        ),
        check_vma=False,
    )
```

profile of v0, /device:TPU:0, one launch (start us, length us, event | category | flops | bytes accessed | tf_op | source)
XLA Modules:
  0.0 1368.6 jit_solution(14719905128942906777)
XLA Ops:
  27.6 218.3 %while.55 = (s32[]{:T(128)}, bf16[352,768]{1,0:T(8,128)(2,1)S(1)}, bf16[4,352,768]{2,1,0:T(8,128)(2,1)}, bf16[4,352,768]{2,1,0:T(8,128)(2,1)}, s32[]{:T(128)}, /...) while((s32[]{:T(128)}, bf16[352,768]{1,0:T(8,128)(2,1)S(1)}, ...), condition=%wide.region_12.13_spmd, body=%wide.region_0.12_spmd.sunk | while | flops 3398127616 | bytes 58575920 | solution.py:292
  32.3 20.2 %conditional.7 = (bf16[352,768]{1,0:T(8,128)(2,1)}) conditional(s32[]{:T(128)} %convert_element_type.348, () %tuple.186, (pred[]{:T(512)}, bf16[352,768]{1,0:T(8,128)(2,1)S(1)}, f32[768]{0:T(1024)S(1)}, f32[768]{0:T(1024)S(1)}, bf16[768,3072]{1,0:T(8,128)(2,1)}, /*index=5*/bf16[3072]{0:T(1024)(128)(2,1)S(1)}, s32[4,352]{1,0:T(4,128)}, s32[]{:T(128)}, ...), branch_computations={%region_1.1_spmd, %region_2.10_spmd} | conditional | flops 3396775936 | bytes 49922208 | solution.py:281
  32.4 20.2 %conditional = (bf16[352,768]{1,0:T(8,128)(2,1)}) conditional(s32[]{:T(128)} %convert_element_type.217, (f32[352,768]{1,0:T(8,128)S(1)}, f32[768]{0:T(1024)S(1)}, f32[768]{0:T(1024)S(1)}, bf16[768,3072]{1,0:T(8,128)(2,1)}, bf16[3072]{0:T(1024)(128)(2,1)S(1)}, /*index=5*/s32[4,352]{1,0:T(4,128)}, s32[]{:T(128)}) %tuple.99, (f32[352,768]{1,0:T(8,128)S(1)}, ...), branch_computations={%region_3.6_spmd, %region_8.9_spmd} | conditional | flops 3396505600 | bytes 48300076 | solution.py:263
  62.4 20.2 %conditional.7 = (bf16[352,768]{1,0:T(8,128)(2,1)}) conditional(s32[]{:T(128)} %convert_element_type.348, () %tuple.186, (pred[]{:T(512)}, bf16[352,768]{1,0:T(8,128)(2,1)S(1)}, f32[768]{0:T(1024)S(1)}, f32[768]{0:T(1024)S(1)}, bf16[768,3072]{1,0:T(8,128)(2,1)}, /*index=5*/bf16[3072]{0:T(1024)(128)(2,1)S(1)}, s32[4,352]{1,0:T(4,128)}, s32[]{:T(128)}, ...), branch_computations={%region_1.1_spmd, %region_2.10_spmd} | conditional | flops 3396775936 | bytes 49922208 | solution.py:281
  62.4 20.2 %conditional = (bf16[352,768]{1,0:T(8,128)(2,1)}) conditional(s32[]{:T(128)} %convert_element_type.217, (f32[352,768]{1,0:T(8,128)S(1)}, f32[768]{0:T(1024)S(1)}, f32[768]{0:T(1024)S(1)}, bf16[768,3072]{1,0:T(8,128)(2,1)}, bf16[3072]{0:T(1024)(128)(2,1)S(1)}, /*index=5*/s32[4,352]{1,0:T(4,128)}, s32[]{:T(128)}) %tuple.99, (f32[352,768]{1,0:T(8,128)S(1)}, ...), branch_computations={%region_3.6_spmd, %region_8.9_spmd} | conditional | flops 3396505600 | bytes 48300076 | solution.py:263
  94.4 20.2 %conditional.7 = (bf16[352,768]{1,0:T(8,128)(2,1)}) conditional(s32[]{:T(128)} %convert_element_type.348, () %tuple.186, (pred[]{:T(512)}, bf16[352,768]{1,0:T(8,128)(2,1)S(1)}, f32[768]{0:T(1024)S(1)}, f32[768]{0:T(1024)S(1)}, bf16[768,3072]{1,0:T(8,128)(2,1)}, /*index=5*/bf16[3072]{0:T(1024)(128)(2,1)S(1)}, s32[4,352]{1,0:T(4,128)}, s32[]{:T(128)}, ...), branch_computations={%region_1.1_spmd, %region_2.10_spmd} | conditional | flops 3396775936 | bytes 49922208 | solution.py:281
  94.4 20.2 %conditional = (bf16[352,768]{1,0:T(8,128)(2,1)}) conditional(s32[]{:T(128)} %convert_element_type.217, (f32[352,768]{1,0:T(8,128)S(1)}, f32[768]{0:T(1024)S(1)}, f32[768]{0:T(1024)S(1)}, bf16[768,3072]{1,0:T(8,128)(2,1)}, bf16[3072]{0:T(1024)(128)(2,1)S(1)}, /*index=5*/s32[4,352]{1,0:T(4,128)}, s32[]{:T(128)}) %tuple.99, (f32[352,768]{1,0:T(8,128)S(1)}, ...), branch_computations={%region_3.6_spmd, %region_8.9_spmd} | conditional | flops 3396505600 | bytes 48300076 | solution.py:263
  124.7 20.2 %conditional.7 = (bf16[352,768]{1,0:T(8,128)(2,1)}) conditional(s32[]{:T(128)} %convert_element_type.348, () %tuple.186, (pred[]{:T(512)}, bf16[352,768]{1,0:T(8,128)(2,1)S(1)}, f32[768]{0:T(1024)S(1)}, f32[768]{0:T(1024)S(1)}, bf16[768,3072]{1,0:T(8,128)(2,1)}, /*index=5*/bf16[3072]{0:T(1024)(128)(2,1)S(1)}, s32[4,352]{1,0:T(4,128)}, s32[]{:T(128)}, ...), branch_computations={%region_1.1_spmd, %region_2.10_spmd} | conditional | flops 3396775936 | bytes 49922208 | solution.py:281
  124.8 20.2 %conditional = (bf16[352,768]{1,0:T(8,128)(2,1)}) conditional(s32[]{:T(128)} %convert_element_type.217, (f32[352,768]{1,0:T(8,128)S(1)}, f32[768]{0:T(1024)S(1)}, f32[768]{0:T(1024)S(1)}, bf16[768,3072]{1,0:T(8,128)(2,1)}, bf16[3072]{0:T(1024)(128)(2,1)S(1)}, /*index=5*/s32[4,352]{1,0:T(4,128)}, s32[]{:T(128)}) %tuple.99, (f32[352,768]{1,0:T(8,128)S(1)}, ...), branch_computations={%region_3.6_spmd, %region_8.9_spmd} | conditional | flops 3396505600 | bytes 48300076 | solution.py:263
  144.9 7.1 collective-permute-start
  161.4 26.5 %collective-permute-start = (bf16[352,768]{1,0:T(8,128)(2,1)}, bf16[352,768]{1,0:T(8,128)(2,1)S(1)}, u32[]{:S(2)}, u32[]{:S(2)}) collective-permute-start(bf16[352,768]{1,0:T(8,128)(2,1)} %get-tuple-element.1913), channel_id=1, source_target_pairs={{0,8},{8,16},{16,24},{1,9},{9,17},{17,25},{2,10},{10,18},{18,26},{... | collective-permute-start | bytes 1622024 | tf_op jit(solution)/shard_map/while/body/eval_jaxpr/ppermute | solution.py:18
  196.1 11.2 collective-permute-start
  215.6 27.5 %collective-permute-start = (bf16[352,768]{1,0:T(8,128)(2,1)}, bf16[352,768]{1,0:T(8,128)(2,1)S(1)}, u32[]{:S(2)}, u32[]{:S(2)}) collective-permute-start(bf16[352,768]{1,0:T(8,128)(2,1)} %get-tuple-element.1913), channel_id=1, source_target_pairs={{0,8},{8,16},{16,24},{1,9},{9,17},{17,25},{2,10},{10,18},{18,26},{... | collective-permute-start | bytes 1622024 | tf_op jit(solution)/shard_map/while/body/eval_jaxpr/ppermute | solution.py:18
  248.4 625.2 %while.56 = (s32[]{:T(128)}, bf16[352,768]{1,0:T(8,128)(2,1)S(1)}, f32[768]{0:T(1024)}, f32[768]{0:T(1024)}, f32[768,3072]{1,0:T(8,128)}, /*index=5*/f32[3072]{0...) while((s32[]{:T(128)}, bf16[352,768]{1,0:T(8,128)(2,1)S(1)}, ...), condition=%wide.region_40.41_spmd.clone, body=%wide.region_13.40_spmd.clone.sunk | while | flops 8410141696 | bytes 260323712 | solution.py:353
  271.5 15.3 %conditional.8 = ((f32[352,768]{1,0:T(8,128)}, f32[768]{0:T(1024)}, f32[768]{0:T(1024)}, f32[768,3072]{1,0:T(8,128)}, f32[3072]{0:T(1024)}, /*index=5*/f32[1536,...) conditional(s32[]{:T(128)} %convert_element_type.349, ...), branch_computations={%region_14.14_spmd, %region_15.37_spmd} | conditional | flops 8399069184 | bytes 193591744 | solution.py:327
  291.5 10.4 select_add_fusion.14
  303.4 8.6 select_add_fusion.16
  317.2 15.3 %conditional.8 = ((f32[352,768]{1,0:T(8,128)}, f32[768]{0:T(1024)}, f32[768]{0:T(1024)}, f32[768,3072]{1,0:T(8,128)}, f32[3072]{0:T(1024)}, /*index=5*/f32[1536,...) conditional(s32[]{:T(128)} %convert_element_type.349, ...), branch_computations={%region_14.14_spmd, %region_15.37_spmd} | conditional | flops 8399069184 | bytes 193591744 | solution.py:327
  337.2 13.1 select_add_fusion.14
  351.8 11.2 select_add_fusion.16
  368.3 15.3 %conditional.8 = ((f32[352,768]{1,0:T(8,128)}, f32[768]{0:T(1024)}, f32[768]{0:T(1024)}, f32[768,3072]{1,0:T(8,128)}, f32[3072]{0:T(1024)}, /*index=5*/f32[1536,...) conditional(s32[]{:T(128)} %convert_element_type.349, ...), branch_computations={%region_14.14_spmd, %region_15.37_spmd} | conditional | flops 8399069184 | bytes 193591744 | solution.py:327
  388.3 13.1 select_add_fusion.14
  402.9 11.2 select_add_fusion.16
  418.7 35.5 %collective-permute-done.1 = bf16[352,768]{1,0:T(8,128)(2,1)S(1)} collective-permute-done((bf16[352,768]{1,0:T(8,128)(2,1)}, bf16[352,768]{1,0:T(8,128)(2,1)S(1)}, u32[]{:S(2)}, u32[]{:S(2)}) %collective-permute-start.1) | collective-permute-done | bytes 540704 | tf_op jit(solution)/shard_map/while/body/eval_jaxpr/ppermute | solution.py:18
  454.9 67.5 %conditional.8 = ((f32[352,768]{1,0:T(8,128)}, f32[768]{0:T(1024)}, f32[768]{0:T(1024)}, f32[768,3072]{1,0:T(8,128)}, f32[3072]{0:T(1024)}, /*index=5*/f32[1536,...) conditional(s32[]{:T(128)} %convert_element_type.349, ...), branch_computations={%region_14.14_spmd, %region_15.37_spmd} | conditional | flops 8399069184 | bytes 193591744 | solution.py:327
  457.1 65.3 %conditional.2 = (f32[352,768]{1,0:T(8,128)}, f32[768]{0:T(1024)}, f32[768]{0:T(1024)}, f32[768,3072]{1,0:T(8,128)}, f32[3072]{0:T(1024)}, /*index=5*/f32[1536,7...) conditional(s32[]{:T(128)} %convert_element_type.250, ...), branch_computations={%region_16.27_spmd, %region_29.36_spmd} | conditional | flops 8398528512 | bytes 190347568 | solution.py:306
  509.3 8.0 pad_maximum_fusion
  527.2 13.1 select_add_fusion.14
  541.8 11.2 select_add_fusion.16
  559.2 67.5 %conditional.8 = ((f32[352,768]{1,0:T(8,128)}, f32[768]{0:T(1024)}, f32[768]{0:T(1024)}, f32[768,3072]{1,0:T(8,128)}, f32[3072]{0:T(1024)}, /*index=5*/f32[1536,...) conditional(s32[]{:T(128)} %convert_element_type.349, ...), branch_computations={%region_14.14_spmd, %region_15.37_spmd} | conditional | flops 8399069184 | bytes 193591744 | solution.py:327
  561.4 65.3 %conditional.2 = (f32[352,768]{1,0:T(8,128)}, f32[768]{0:T(1024)}, f32[768]{0:T(1024)}, f32[768,3072]{1,0:T(8,128)}, f32[3072]{0:T(1024)}, /*index=5*/f32[1536,7...) conditional(s32[]{:T(128)} %convert_element_type.250, ...), branch_computations={%region_16.27_spmd, %region_29.36_spmd} | conditional | flops 8398528512 | bytes 190347568 | solution.py:306
  613.6 8.0 pad_maximum_fusion
  631.5 13.1 select_add_fusion.14
  646.1 11.2 select_add_fusion.16
  663.5 67.5 %conditional.8 = ((f32[352,768]{1,0:T(8,128)}, f32[768]{0:T(1024)}, f32[768]{0:T(1024)}, f32[768,3072]{1,0:T(8,128)}, f32[3072]{0:T(1024)}, /*index=5*/f32[1536,...) conditional(s32[]{:T(128)} %convert_element_type.349, ...), branch_computations={%region_14.14_spmd, %region_15.37_spmd} | conditional | flops 8399069184 | bytes 193591744 | solution.py:327
  665.7 65.3 %conditional.2 = (f32[352,768]{1,0:T(8,128)}, f32[768]{0:T(1024)}, f32[768]{0:T(1024)}, f32[768,3072]{1,0:T(8,128)}, f32[3072]{0:T(1024)}, /*index=5*/f32[1536,7...) conditional(s32[]{:T(128)} %convert_element_type.250, ...), branch_computations={%region_16.27_spmd, %region_29.36_spmd} | conditional | flops 8398528512 | bytes 190347568 | solution.py:306
  717.9 8.0 pad_maximum_fusion
  735.8 13.1 select_add_fusion.14
  750.4 11.2 select_add_fusion.16
  767.8 67.5 %conditional.8 = ((f32[352,768]{1,0:T(8,128)}, f32[768]{0:T(1024)}, f32[768]{0:T(1024)}, f32[768,3072]{1,0:T(8,128)}, f32[3072]{0:T(1024)}, /*index=5*/f32[1536,...) conditional(s32[]{:T(128)} %convert_element_type.349, ...), branch_computations={%region_14.14_spmd, %region_15.37_spmd} | conditional | flops 8399069184 | bytes 193591744 | solution.py:327
  770.0 65.3 %conditional.2 = (f32[352,768]{1,0:T(8,128)}, f32[768]{0:T(1024)}, f32[768]{0:T(1024)}, f32[768,3072]{1,0:T(8,128)}, f32[3072]{0:T(1024)}, /*index=5*/f32[1536,7...) conditional(s32[]{:T(128)} %convert_element_type.250, ...), branch_computations={%region_16.27_spmd, %region_29.36_spmd} | conditional | flops 8398528512 | bytes 190347568 | solution.py:306
  822.2 8.0 pad_maximum_fusion
  840.1 13.1 select_add_fusion.14
  854.7 11.2 select_add_fusion.16
  888.5 69.2 %psum.42 = f32[768]{0:T(1024)} all-reduce(f32[768]{0:T(1024)S(1)} %copy-done.34), channel_id=1, replica_groups=mesh['section'=4,'dp'=8] {'section','dp'}, use_global_device_ids=true, to_apply=%region_41.42 | all-reduce | flops 768 | bytes 6144 | tf_op jit(solution)/shard_map/psum | solution.py:368
  957.7 39.7 %all-reduce.1 = (f32[1,768]{1,0:T(1,128)}, f32[1,768]{1,0:T(1,128)}, f32[1,3072]{1,0:T(1,128)}) all-reduce(f32[1,768]{1,0:T(1,128)S(1)} %broadcast_in_dim.190, f32[1,768]{1,0:T(1,128)S(1)} %broadcast_in_dim.191, f32[1,3072]{1,0:T(1,128)S(1)} %bitcast.137), channel_id=1, replica_groups=mesh['section'=4,'dp'=8] {'dp'}, use_global_device_ids=true, to_apply=%region_42.43 | all-reduce | flops 4608 | bytes 36864 | tf_op jit(solution)/shard_map/psum | solution.py:365
  997.5 353.2 %all-reduce.5.cloned.1.call-done = (f32[1,768,3072]{2,1,0:T(8,128)}, f32[1,1536,768]{2,1,0:T(8,128)}) async-done(((f32[1,768,3072]{2,1,0:T(8,128)}, f32[1,1536,768]{2,1,0:T(8,128)}), (f32[1,768,3072]{2,1,0:T(8,128)}, f32[1,1536,768]{2,1,0:T(8,128)})) %all-reduce.5.cloned.1.call-update) | async-done | bytes 14155792 | tf_op jit(solution)/shard_map/psum | solution.py:365
  1350.6 8.8 copy.149
  (770 shorter events, 552.5 us)
Async XLA Ops:
  7.2 13.3 copy-start.16
  7.2 1343.5 %all-reduce.5.cloned.1.call-start = ((), (), s32[]{:S(2)}) async-start(), calls=%async_computation | async-start | bytes 28311552 | tf_op jit(solution)/shard_map/psum | solution.py:365
  7.2 13.2 collective-permute-start.2
  11.8 12.8 collective-permute-start.3
  52.6 5.1 collective-permute-start
  82.6 7.1 collective-permute-start
  114.6 5.4 collective-permute-start
  144.9 10.9 collective-permute-start
  161.4 29.2 %collective-permute-start = (bf16[352,768]{1,0:T(8,128)(2,1)}, bf16[352,768]{1,0:T(8,128)(2,1)S(1)}, u32[]{:S(2)}, u32[]{:S(2)}) collective-permute-start(bf16[352,768]{1,0:T(8,128)(2,1)} %get-tuple-element.1913), channel_id=1, source_target_pairs={{0,8},{8,16},{16,24},{1,9},{9,17},{17,25},{2,10},{10,18},{18,26},{... | collective-permute-start | bytes 1622024 | tf_op jit(solution)/shard_map/while/body/eval_jaxpr/ppermute | solution.py:18
  196.1 13.9 %collective-permute-start = (bf16[352,768]{1,0:T(8,128)(2,1)}, bf16[352,768]{1,0:T(8,128)(2,1)S(1)}, u32[]{:S(2)}, u32[]{:S(2)}) collective-permute-start(bf16[352,768]{1,0:T(8,128)(2,1)} %get-tuple-element.1913), channel_id=1, source_target_pairs={{0,8},{8,16},{16,24},{1,9},{9,17},{17,25},{2,10},{10,18},{18,26},{... | collective-permute-start | bytes 1622024 | tf_op jit(solution)/shard_map/while/body/eval_jaxpr/ppermute | solution.py:18
  215.6 30.3 %collective-permute-start = (bf16[352,768]{1,0:T(8,128)(2,1)}, bf16[352,768]{1,0:T(8,128)(2,1)S(1)}, u32[]{:S(2)}, u32[]{:S(2)}) collective-permute-start(bf16[352,768]{1,0:T(8,128)(2,1)} %get-tuple-element.1913), channel_id=1, source_target_pairs={{0,8},{8,16},{16,24},{1,9},{9,17},{17,25},{2,10},{10,18},{18,26},{... | collective-permute-start | bytes 1622024 | tf_op jit(solution)/shard_map/while/body/eval_jaxpr/ppermute | solution.py:18
  286.8 29.7 %collective-permute-start.1 = (bf16[352,768]{1,0:T(8,128)(2,1)}, bf16[352,768]{1,0:T(8,128)(2,1)S(1)}, u32[]{:S(2)}, u32[]{:S(2)}) collective-permute-start(bf16[352,768]{1,0:T(8,128)(2,1)} %get-tuple-element.1693), channel_id=1, source_target_pairs={{8,0},{16,8},{24,16},{9,1},{17,9},{25,17},{10,2},{18,10},{26,18},{... | collective-permute-start | bytes 1622024 | tf_op jit(solution)/shard_map/while/body/eval_jaxpr/ppermute | solution.py:18
  332.5 35.1 %collective-permute-start.1 = (bf16[352,768]{1,0:T(8,128)(2,1)}, bf16[352,768]{1,0:T(8,128)(2,1)S(1)}, u32[]{:S(2)}, u32[]{:S(2)}) collective-permute-start(bf16[352,768]{1,0:T(8,128)(2,1)} %get-tuple-element.1693), channel_id=1, source_target_pairs={{8,0},{16,8},{24,16},{9,1},{17,9},{25,17},{10,2},{18,10},{26,18},{... | collective-permute-start | bytes 1622024 | tf_op jit(solution)/shard_map/while/body/eval_jaxpr/ppermute | solution.py:18
  337.2 13.2 copy-start.20
  337.2 13.9 %copy-start.36 = (s32[3]{0:T(128)S(1)}, s32[3]{0:T(128)}, u32[]{:S(2)}) copy-start(s32[3]{0:T(128)} %get-tuple-element.1900) | copy-start | bytes 40 | tf_op jit(solution)/shard_map/while
  351.8 12.0 copy-start.29
  351.8 12.0 copy-start.32
  383.6 70.6 %collective-permute-start.1 = (bf16[352,768]{1,0:T(8,128)(2,1)}, bf16[352,768]{1,0:T(8,128)(2,1)S(1)}, u32[]{:S(2)}, u32[]{:S(2)}) collective-permute-start(bf16[352,768]{1,0:T(8,128)(2,1)} %get-tuple-element.1693), channel_id=1, source_target_pairs={{8,0},{16,8},{24,16},{9,1},{17,9},{25,17},{10,2},{18,10},{26,18},{... | collective-permute-start | bytes 1622024 | tf_op jit(solution)/shard_map/while/body/eval_jaxpr/ppermute | solution.py:18
  388.3 13.2 copy-start.20
  388.3 13.9 %copy-start.36 = (s32[3]{0:T(128)S(1)}, s32[3]{0:T(128)}, u32[]{:S(2)}) copy-start(s32[3]{0:T(128)} %get-tuple-element.1900) | copy-start | bytes 40 | tf_op jit(solution)/shard_map/while
  402.9 12.0 copy-start.29
  402.9 12.0 copy-start.32
  414.1 40.1 %copy-start.4 = (f32[768]{0:T(1024)S(1)}, f32[768]{0:T(1024)}, u32[]{:S(2)}) copy-start(f32[768]{0:T(1024)} %copy-done.3) | copy-start | bytes 9220 | tf_op jit(solution)/shard_map/while
  414.1 40.1 %copy-start.8 = (f32[768]{0:T(1024)S(1)}, f32[768]{0:T(1024)}, u32[]{:S(2)}) copy-start(f32[768]{0:T(1024)} %copy-done.7) | copy-start | bytes 9220 | tf_op jit(solution)/shard_map/while
  414.1 40.1 %copy-start.18 = (bf16[3072]{0:T(1024)(128)(2,1)S(1)}, bf16[3072]{0:T(1024)(128)(2,1)}, u32[]{:S(2)}) copy-start(bf16[3072]{0:T(1024)(128)(2,1)} %copy-done.17) | copy-start | bytes 18436 | tf_op jit(solution)/shard_map/while
  414.9 39.4 %copy-start.24 = (f32[768]{0:T(1024)}, f32[768]{0:T(1024)S(1)}, u32[]{:S(2)}) copy-start(f32[768]{0:T(1024)S(1)} %get-tuple-element.1874) | copy-start | bytes 9220 | tf_op jit(solution)/shard_map/while
  414.9 39.4 %copy-start.27 = (f32[768]{0:T(1024)}, f32[768]{0:T(1024)S(1)}, u32[]{:S(2)}) copy-start(f32[768]{0:T(1024)S(1)} %get-tuple-element.1875) | copy-start | bytes 9220 | tf_op jit(solution)/shard_map/while
  415.6 38.6 %copy-start.30 = (f32[768]{0:T(1024)}, f32[768]{0:T(1024)S(1)}, u32[]{:S(2)}) copy-start(f32[768]{0:T(1024)S(1)} %get-tuple-element.1880) | copy-start | bytes 9220 | tf_op jit(solution)/shard_map/while
  415.6 38.6 %copy-start.33 = (f32[768]{0:T(1024)}, f32[768]{0:T(1024)S(1)}, u32[]{:S(2)}) copy-start(f32[768]{0:T(1024)S(1)} %get-tuple-element.1882) | copy-start | bytes 9220 | tf_op jit(solution)/shard_map/while
  522.4 36.1 %collective-permute-start.1 = (bf16[352,768]{1,0:T(8,128)(2,1)}, bf16[352,768]{1,0:T(8,128)(2,1)S(1)}, u32[]{:S(2)}, u32[]{:S(2)}) collective-permute-start(bf16[352,768]{1,0:T(8,128)(2,1)} %get-tuple-element.1693), channel_id=1, source_target_pairs={{8,0},{16,8},{24,16},{9,1},{17,9},{25,17},{10,2},{18,10},{26,18},{... | collective-permute-start | bytes 1622024 | tf_op jit(solution)/shard_map/while/body/eval_jaxpr/ppermute | solution.py:18
  527.2 13.2 copy-start.20
  527.2 13.9 %copy-start.36 = (s32[3]{0:T(128)S(1)}, s32[3]{0:T(128)}, u32[]{:S(2)}) copy-start(s32[3]{0:T(128)} %get-tuple-element.1900) | copy-start | bytes 40 | tf_op jit(solution)/shard_map/while
  541.8 12.0 copy-start.32
  626.7 36.1 %collective-permute-start.1 = (bf16[352,768]{1,0:T(8,128)(2,1)}, bf16[352,768]{1,0:T(8,128)(2,1)S(1)}, u32[]{:S(2)}, u32[]{:S(2)}) collective-permute-start(bf16[352,768]{1,0:T(8,128)(2,1)} %get-tuple-element.1693), channel_id=1, source_target_pairs={{8,0},{16,8},{24,16},{9,1},{17,9},{25,17},{10,2},{18,10},{26,18},{... | collective-permute-start | bytes 1622024 | tf_op jit(solution)/shard_map/while/body/eval_jaxpr/ppermute | solution.py:18
  631.5 13.2 copy-start.20
  631.5 13.9 %copy-start.36 = (s32[3]{0:T(128)S(1)}, s32[3]{0:T(128)}, u32[]{:S(2)}) copy-start(s32[3]{0:T(128)} %get-tuple-element.1900) | copy-start | bytes 40 | tf_op jit(solution)/shard_map/while
  646.1 12.0 copy-start.32
  731.0 36.1 %collective-permute-start.1 = (bf16[352,768]{1,0:T(8,128)(2,1)}, bf16[352,768]{1,0:T(8,128)(2,1)S(1)}, u32[]{:S(2)}, u32[]{:S(2)}) collective-permute-start(bf16[352,768]{1,0:T(8,128)(2,1)} %get-tuple-element.1693), channel_id=1, source_target_pairs={{8,0},{16,8},{24,16},{9,1},{17,9},{25,17},{10,2},{18,10},{26,18},{... | collective-permute-start | bytes 1622024 | tf_op jit(solution)/shard_map/while/body/eval_jaxpr/ppermute | solution.py:18
  735.8 13.2 copy-start.20
  735.8 13.9 %copy-start.36 = (s32[3]{0:T(128)S(1)}, s32[3]{0:T(128)}, u32[]{:S(2)}) copy-start(s32[3]{0:T(128)} %get-tuple-element.1900) | copy-start | bytes 40 | tf_op jit(solution)/shard_map/while
  750.4 12.0 copy-start.32
  835.3 35.1 %collective-permute-start.1 = (bf16[352,768]{1,0:T(8,128)(2,1)}, bf16[352,768]{1,0:T(8,128)(2,1)S(1)}, u32[]{:S(2)}, u32[]{:S(2)}) collective-permute-start(bf16[352,768]{1,0:T(8,128)(2,1)} %get-tuple-element.1693), channel_id=1, source_target_pairs={{8,0},{16,8},{24,16},{9,1},{17,9},{25,17},{10,2},{18,10},{26,18},{... | collective-permute-start | bytes 1622024 | tf_op jit(solution)/shard_map/while/body/eval_jaxpr/ppermute | solution.py:18
  840.1 13.2 copy-start.20
  840.1 13.9 %copy-start.36 = (s32[3]{0:T(128)S(1)}, s32[3]{0:T(128)}, u32[]{:S(2)}) copy-start(s32[3]{0:T(128)} %get-tuple-element.1900) | copy-start | bytes 40 | tf_op jit(solution)/shard_map/while
  854.7 12.0 copy-start.32
  876.3 7.5 collective-permute-start.5
  886.5 71.3 %copy-start.22 = (f32[3072]{0:T(1024)S(1)}, f32[3072]{0:T(1024)}, u32[]{:S(2)}) copy-start(f32[3072]{0:T(1024)} %get-tuple-element.1209) | copy-start | bytes 36868
  887.1 70.6 %collective-permute-start.4 = (bf16[768]{0:T(1024)(128)(2,1)S(1)}, bf16[768]{0:T(1024)(128)(2,1)S(1)}, u32[]{:S(2)}, u32[]{:S(2)}) collective-permute-start(bf16[768]{0:T(1024)(128)(2,1)S(1)} %convert_element_type.267), channel_id=1, source_target_pairs={{8,0},{16,8},{24,16},{9,1},{17,9},{25,17},{10,2},{18,10},{26,18},{... | collective-permute-start | bytes 4616 | tf_op jit(solution)/shard_map/ppermute | solution.py:18
  (151 other events, 741.1 us)
Sparse Core Ops, SparseCore 0:
  886.6 463.9 all-reduce.4
where the time goes:
time: 1390 us; the launch traced here: 1370 us
  waiting for transfers between devices  398 us (29%)
  other arithmetic  355 us (26%)
  matrix products  195 us (14%)
  local copies, waits for them, and re-layouts  171 us (12%)
  blocking collectives  109 us (8%)
  starting transfers between devices  97.1 us (7%)
  loops' own time  28.3 us (2%)
  between operations  14.4 us (1%)
    psum x1, waiting for transfers between devices, shards(): lax.psum((grad_gain, grad_shift, grad_first, grad_bias, grad_half), 'dp')  353 us
    add x28, other arithmetic, backward_step(): running + addend  175 us
    ppermute x18, starting transfers between devices, from_behind(): lax.ppermute(value, axis, [(source, source + steps) for source in range(i...  97.1 us
    psum x1, blocking collectives, shards(): token_grad = lax.psum(token_total, ('section', 'dp'))  69.2 us
    another operation x39, local copies, waits for them, and re-layouts  54.9 us
    ppermute x18, waiting for transfers between devices, from_behind(): lax.ppermute(value, axis, [(source, source + steps) for source in range(i...  44.6 us
    sub x8, matrix products, attention_weights(): raised = jnp.exp(scores - row_max)  39.7 us
    psum x1, blocking collectives, shards(): lax.psum((grad_gain, grad_shift, grad_first, grad_bias, grad_half), 'dp')  39.7 us
  transfers between devices with their start and end apart: 19, of which 6 were waited for; matrix products, arithmetic and copies ran while one was open for 19% of the time, Pallas kernels for 0%

commit v1 on v0

v1 whole, which is shorter than its diff:
```python
from functools import partial

import jax
import jax.numpy as jnp
import numpy as np
from jax import lax
from jax.experimental import pallas as pl
from jax.experimental.pallas import tpu as pltpu
from jax.sharding import PartitionSpec as P

HEADS = 12
EPSILON = 1e-06
NEGATIVE = -1000000000.0
GROUP = 256
TILE = 512
VMEM_LIMIT = 60 * 1024 * 1024
BF16 = jnp.bfloat16
F32 = jnp.float32
ANY = pl.BlockSpec(memory_space=pl.ANY)
SMEM = pl.BlockSpec(memory_space=pltpu.SMEM)
VMEM = pl.BlockSpec(memory_space=pltpu.VMEM)


def dot_nn(a, b):
    return jnp.dot(a, b, preferred_element_type=F32)


def dot_nt(a, b):
    return lax.dot_general(a, b, (((1,), (1,)), ((), ())), preferred_element_type=F32)


def dot_tn(a, b):
    return lax.dot_general(a, b, (((0,), (0,)), ((), ())), preferred_element_type=F32)


def fetch(choice, first, second, target, sem):
    @pl.when(choice)
    def _():
        pltpu.make_async_copy(first, target, sem).start()

    @pl.when(jnp.logical_not(choice))
    def _():
        pltpu.make_async_copy(second, target, sem).start()

    return pltpu.make_async_copy(first, target, sem)


def deliver(choice, source, first, second, sem):
    @pl.when(choice)
    def _():
        pltpu.make_async_copy(source, first, sem).start()

    @pl.when(jnp.logical_not(choice))
    def _():
        pltpu.make_async_copy(source, second, sem).start()

    return pltpu.make_async_copy(source, first, sem)


def start_copy(source, target, sem):
    copy = pltpu.make_async_copy(source, target, sem)
    copy.start()
    return copy


def norm_parts(x):
    centred = x - jnp.mean(x, -1, keepdims=True)
    scale = lax.rsqrt(jnp.mean(centred * centred, -1, keepdims=True) + EPSILON)
    return centred * scale, scale


def gelu_pair(hidden):
    z = jnp.abs(hidden) * 0.7071067811865476
    t = 1.0 / (1.0 + 0.3275911 * z)
    poly = ((((1.061405429 * t - 1.453152027) * t + 1.421413741) * t - 0.284496736) * t + 0.254829592) * t
    fall = jnp.exp(-z * z)
    tail = 0.5 * poly * fall
    cdf = jnp.where(hidden >= 0, 1.0 - tail, tail)
    return hidden * cdf, cdf + hidden * fall * 0.3989422804014327


def columns(index, width):
    return pl.ds(pl.multiple_of(index * width, width), width)


def head_mask(rows, head):
    lane = lax.broadcasted_iota(jnp.int32, (rows, GROUP), 1)
    return (lane >= head * 64) & (lane < head * 64 + 64)


def load_weights(core_even, first_own, first_other, half_own, half_other, w_att, w_up, w_down, sems):
    half = half_own.shape[0]
    return (
        fetch(core_even, first_own, first_other, w_att, sems.at[0]),
        fetch(core_even, first_other, first_own, w_up, sems.at[1]),
        fetch(core_even, half_own, half_other, w_down.at[pl.ds(0, half)], sems.at[2]),
        fetch(core_even, half_other, half_own, w_down.at[pl.ds(half, half)], sems.at[3]),
    )


def forward_kernel(
    place, start_row, sent_row, vec_att, vec_mlp, seg_row, seg_col, first_own, first_other, half_own, half_other,
    keep_out, send_out, y_mlp_out, x_out, mid_out, qkv_out, soft_out, ctx_out, act_out, slope_out,
    w_att, w_up, w_down, x, bias, normed, qkv, soft, ctx, mid, act, slope, y_mlp, sems,
):
    core_even = place[0] == 0
    early = place[1] == 0
    rows, width = x.shape
    groups = width // GROUP
    get_x = fetch(early, start_row, sent_row, x, sems.at[4])
    get_att, get_up, get_low, get_high = load_weights(
        core_even, first_own, first_other, half_own, half_other, w_att, w_up, w_down, sems
    )
    bias[...] = jnp.where(seg_col[...] == seg_row[...], 0.0, NEGATIVE)
    get_x.wait()
    put_x = start_copy(x, x_out, sems.at[5])
    hat, _ = norm_parts(x[...].astype(F32))
    normed[...] = (hat * vec_att[0:1] + vec_att[1:2]).astype(BF16)
    get_att.wait()

    def group_step(group, carry):
        low = normed[...]
        cols = columns(group, GROUP)
        k_cols = pl.ds(pl.multiple_of(width + group * GROUP, GROUP), GROUP)
        v_cols = pl.ds(pl.multiple_of(2 * width + group * GROUP, GROUP), GROUP)
        q = ((dot_nn(low, w_att[:, cols]) + vec_att[2:3, cols]).astype(BF16) * 0.125).astype(BF16)
        k = dot_nn(low, w_att[:, k_cols]).astype(BF16)
        v = (dot_nn(low, w_att[:, v_cols]) + vec_att[3:4, cols]).astype(BF16)
        qkv[:, cols] = q
        qkv[:, k_cols] = k
        qkv[:, v_cols] = v
        total = jnp.zeros((rows, GROUP), F32)
        for head in range(GROUP // 64):
            mask = head_mask(rows, head)
            scores = dot_nt(jnp.where(mask, q, 0), k) + bias[...]
            raised = jnp.exp(scores - jnp.max(scores, -1, keepdims=True))
            weight = (raised * (1.0 / jnp.sum(raised, -1, keepdims=True))).astype(BF16)
            soft[group * (GROUP // 64) + head] = weight
            total = total + dot_nn(weight, jnp.where(mask, v, 0))
        ctx[:, cols] = total.astype(BF16)
        return carry

    lax.fori_loop(0, groups, group_step, 0)
    put_qkv = start_copy(qkv, qkv_out, sems.at[6])
    put_soft = start_copy(soft, soft_out, sems.at[7])
    put_ctx = start_copy(ctx, ctx_out, sems.at[8])
    y = x[...].astype(F32) + dot_nn(ctx[...], w_att[:, 3 * width :]) + vec_att[4:5]
    low = y.astype(BF16)
    mid[...] = low
    put_mid = start_copy(mid, mid_out, sems.at[9])
    put_first = deliver(core_even, mid, keep_out, send_out, sems.at[10])
    hat, _ = norm_parts(low.astype(F32))
    normed[...] = (hat * vec_mlp[0:1, :width] + vec_mlp[1:2, :width]).astype(BF16)
    get_up.wait()

    def up_step(tile, carry):
        cols = columns(tile, TILE)
        hidden = dot_nn(normed[...], w_up[:, cols]) + vec_mlp_bias(vec_mlp, tile)
        active, rate = gelu_pair(hidden)
        act[:, cols] = active.astype(BF16)
        slope[:, cols] = rate.astype(BF16)
        return carry

    lax.fori_loop(0, act.shape[1] // TILE, up_step, 0)
    put_act = start_copy(act, act_out, sems.at[11])
    put_slope = start_copy(slope, slope_out, sems.at[12])
    get_low.wait()
    get_high.wait()

    def down_step(group, carry):
        cols = columns(group, GROUP)
        y_mlp[:, cols] = (
            mid[:, cols].astype(F32) + dot_nn(act[...], w_down[:, cols]) + vec_att[5:6, cols]
        ).astype(BF16)
        return carry

    lax.fori_loop(0, groups, down_step, 0)
    put_y = start_copy(y_mlp, y_mlp_out, sems.at[13])
    put_second = deliver(core_even, y_mlp, send_out, keep_out, sems.at[14])
    for put in (put_x, put_qkv, put_soft, put_ctx, put_mid, put_first, put_act, put_slope, put_y, put_second):
        put.wait()


def vec_mlp_bias(vec_mlp, tile):
    return vec_mlp[6:7, columns(tile, TILE)]


def forward_call(place, start_row, sent_row, vec_att, vec_mlp, seg_row, seg_col, weights):
    rows, width = start_row.shape
    hidden = weights[0].shape[1]
    low = lambda *shape: jax.ShapeDtypeStruct(shape, BF16)
    row = low(rows, width)
    outs = [row, row, row, row, row, low(rows, 3 * width), low(HEADS, rows, rows), row, low(rows, hidden), low(rows, hidden)]
    v = pltpu.VMEM
    return pl.pallas_call(
        forward_kernel,
        out_shape=outs,
        in_specs=[SMEM, ANY, ANY, VMEM, VMEM, VMEM, VMEM, ANY, ANY, ANY, ANY],
        out_specs=[ANY] * len(outs),
        scratch_shapes=[
            v((width, hidden), BF16), v((width, hidden), BF16), v((hidden, width), BF16),
            v((rows, width), BF16), v((rows, rows), F32), v((rows, width), BF16),
            v((rows, 3 * width), BF16), v((HEADS, rows, rows), BF16), v((rows, width), BF16), v((rows, width), BF16),
            v((rows, hidden), BF16), v((rows, hidden), BF16), v((rows, width), BF16),
            pltpu.SemaphoreType.DMA((15,)),
        ],
        compiler_params=pltpu.CompilerParams(vmem_limit_bytes=VMEM_LIMIT),
        cost_estimate=pl.CostEstimate(flops=7_000_000_000, bytes_accessed=26_000_000, transcendentals=2_500_000),
        name="row_forward",
    )(place, start_row, sent_row, vec_att, vec_mlp, seg_row, seg_col, *weights)


def backward_kernel(
    place, cot_row, back_row, vec_att, vec_mlp, mask_col, first_own, first_other, half_own, half_other,
    x_a, mid_a, qkv_a, soft_a, ctx_a, slope_a, x_b, mid_b, qkv_b, soft_b, ctx_b, slope_b,
    keep_out, send_out, grad_x_out, small_out, norm_att_out, norm_mlp_out, dqkv_out, dhid_out, gmid_out, grad_y_out,
    w_att, w_up, w_down, grad_y, x, mid, qkv, soft, ctx, slope, normed_att, normed_mlp, dqkv, dhid, gmid, gx, dn, sems,
):
    core_even = place[0] == 0
    early = place[1] == 0
    rows, width = x.shape
    groups = width // GROUP

    @pl.when(place[2] == 0)
    def _():
        small_out[...] = jnp.zeros(small_out.shape, F32)

    @pl.when(place[2] == 1)
    def _():
        get_g = fetch(early, back_row, cot_row, grad_y, sems.at[4])
        get_att, get_up, get_low, get_high = load_weights(
            core_even, first_own, first_other, half_own, half_other, w_att, w_up, w_down, sems
        )
        get_slope = fetch(early, slope_a, slope_b, slope, sems.at[5])
        get_mid = fetch(early, mid_a, mid_b, mid, sems.at[6])
        get_x = fetch(early, x_a, x_b, x, sems.at[7])
        get_qkv = fetch(early, qkv_a, qkv_b, qkv, sems.at[8])
        get_soft = fetch(early, soft_a, soft_b, soft, sems.at[9])
        get_ctx = fetch(early, ctx_a, ctx_b, ctx, sems.at[10])
        small_out[...] = jnp.zeros(small_out.shape, F32)
        get_g.wait()
        put_gy = start_copy(grad_y, grad_y_out, sems.at[11])
        get_low.wait()
        get_high.wait()
        get_slope.wait()
        small_out[5:6, :width] = jnp.sum(grad_y[...].astype(F32), 0, keepdims=True)

        def hid_step(tile, carry):
            cols = columns(tile, TILE)
            grad = dot_nt(grad_y[...], w_down[cols, :]) * slope[:, cols].astype(F32)
            low = grad.astype(BF16)
            dhid[:, cols] = low
            small_out[13:14, cols] = jnp.sum(low.astype(F32), 0, keepdims=True)
            return carry

        lax.fori_loop(0, dhid.shape[1] // TILE, hid_step, 0)
        put_dhid = start_copy(dhid, dhid_out, sems.at[12])
        get_up.wait()

        def up_back(group, carry):
            cols = columns(group, GROUP)
            dn[:, cols] = dot_nt(dhid[...], w_up[cols, :])
            return carry

        lax.fori_loop(0, groups, up_back, 0)
        get_mid.wait()
        hat, scale = norm_parts(mid[...].astype(F32))
        normed_mlp[...] = (hat * vec_mlp[0:1, :width] + vec_mlp[1:2, :width]).astype(BF16)
        put_nm = start_copy(normed_mlp, norm_mlp_out, sems.at[13])
        dnorm = dn[...]
        small_out[6:7, :width] = jnp.sum(dnorm * hat, 0, keepdims=True)
        small_out[7:8, :width] = jnp.sum(dnorm, 0, keepdims=True)
        u = dnorm * vec_mlp[0:1, :width]
        grad = grad_y[...].astype(F32) + scale * (
            u - jnp.mean(u, -1, keepdims=True) - hat * jnp.mean(u * hat, -1, keepdims=True)
        )
        low = grad.astype(BF16)
        gmid[...] = low
        put_gmid = start_copy(gmid, gmid_out, sems.at[14])
        put_first = deliver(core_even, gmid, send_out, keep_out, sems.at[15])
        small_out[4:5, :width] = jnp.sum(low.astype(F32), 0, keepdims=True)
        get_att.wait()
        get_qkv.wait()
        get_soft.wait()
        get_ctx.wait()

        def group_step(group, carry):
            cols = columns(group, GROUP)
            k_cols = pl.ds(pl.multiple_of(width + group * GROUP, GROUP), GROUP)
            v_cols = pl.ds(pl.multiple_of(2 * width + group * GROUP, GROUP), GROUP)
            dctx = dot_nt(gmid[...], w_att[cols, 3 * width :]).astype(BF16)
            q = qkv[:, cols]
            k = qkv[:, k_cols]
            v = qkv[:, v_cols]
            product = dctx.astype(F32) * ctx[:, cols].astype(F32)
            dq = jnp.zeros((rows, GROUP), F32)
            dk = jnp.zeros((rows, GROUP), F32)
            dv = jnp.zeros((rows, GROUP), F32)
            for head in range(GROUP // 64):
                mask = head_mask(rows, head)
                weight = soft[group * (GROUP // 64) + head]
                mine = jnp.where(mask, dctx, 0)
                delta = jnp.sum(jnp.where(mask, product, 0.0), -1, keepdims=True)
                ds = (weight.astype(F32) * (dot_nt(mine, v) - delta)).astype(BF16)
                dq = dq + dot_nn(ds, jnp.where(mask, k, 0))
                dk = dk + dot_tn(ds, jnp.where(mask, q, 0))
                dv = dv + dot_tn(weight, mine)
            dq_low = (dq * 0.125).astype(BF16)
            dv_low = dv.astype(BF16)
            dqkv[:, cols] = dq_low
            dqkv[:, k_cols] = dk.astype(BF16)
            dqkv[:, v_cols] = dv_low
            small_out[2:3, cols] = jnp.sum(dq_low.astype(F32), 0, keepdims=True)
            small_out[3:4, cols] = jnp.sum(dv_low.astype(F32), 0, keepdims=True)
            return carry

        lax.fori_loop(0, groups, group_step, 0)
        put_dqkv = start_copy(dqkv, dqkv_out, sems.at[16])

        def qkv_back(group, carry):
            cols = columns(group, GROUP)
            dn[:, cols] = dot_nt(dqkv[...], w_att[cols, : 3 * width])
            return carry

        lax.fori_loop(0, groups, qkv_back, 0)
        get_x.wait()
        hat, scale = norm_parts(x[...].astype(F32))
        normed_att[...] = (hat * vec_att[0:1] + vec_att[1:2]).astype(BF16)
        put_na = start_copy(normed_att, norm_att_out, sems.at[17])
        dnorm = dn[...]
        small_out[0:1, :width] = jnp.sum(dnorm * hat, 0, keepdims=True)
        small_out[1:2, :width] = jnp.sum(dnorm, 0, keepdims=True)
        u = dnorm * vec_att[0:1]
        grad = gmid[...].astype(F32) + scale * (
            u - jnp.mean(u, -1, keepdims=True) - hat * jnp.mean(u * hat, -1, keepdims=True)
        )
        small_out[12:13, :width] = jnp.sum(jnp.where(mask_col[...] == 1, grad, 0.0), 0, keepdims=True)
        gx[...] = grad.astype(BF16)
        put_gx = start_copy(gx, grad_x_out, sems.at[18])
        put_second = deliver(core_even, gx, keep_out, send_out, sems.at[19])
        for put in (put_gy, put_dhid, put_nm, put_gmid, put_first, put_dqkv, put_na, put_gx, put_second):
            put.wait()


def backward_call(place, cot_row, back_row, vec_att, vec_mlp, mask_col, weights, saved_early, saved_late):
    rows, width = cot_row.shape
    hidden = weights[0].shape[1]
    low = lambda *shape: jax.ShapeDtypeStruct(shape, BF16)
    row = low(rows, width)
    outs = [row, row, row, jax.ShapeDtypeStruct((16, hidden), F32), row, row, low(rows, 3 * width), low(rows, hidden), row, row]
    specs = [ANY] * len(outs)
    specs[3] = VMEM
    v = pltpu.VMEM
    return pl.pallas_call(
        backward_kernel,
        out_shape=outs,
        in_specs=[SMEM, ANY, ANY, VMEM, VMEM, VMEM] + [ANY] * 16,
        out_specs=specs,
        scratch_shapes=[
            v((width, hidden), BF16), v((width, hidden), BF16), v((hidden, width), BF16),
            v((rows, width), BF16), v((rows, width), BF16), v((rows, width), BF16),
            v((rows, 3 * width), BF16), v((HEADS, rows, rows), BF16), v((rows, width), BF16), v((rows, hidden), BF16),
            v((rows, width), BF16), v((rows, width), BF16), v((rows, 3 * width), BF16), v((rows, hidden), BF16),
            v((rows, width), BF16), v((rows, width), BF16), v((rows, width), F32),
            pltpu.SemaphoreType.DMA((20,)),
        ],
        compiler_params=pltpu.CompilerParams(vmem_limit_bytes=VMEM_LIMIT),
        cost_estimate=pl.CostEstimate(flops=8_000_000_000, bytes_accessed=34_000_000, transcendentals=1_000),
        name="row_backward",
    )(place, cot_row, back_row, vec_att, vec_mlp, mask_col, *weights, *saved_early, *saved_late)


def weight_kernel(count, place, *refs):
    per_row = 8
    sources = refs[: 2 * count * per_row]
    own_first, own_half, other_first, other_half = refs[2 * count * per_row : 2 * count * per_row + 4]
    (na, nm, dqkv, dhid, ctx, act, gmid, gy, na_t, nm_t, ctx_t, grad_att, grad_up, grad_low, grad_high, sems) = refs[
        2 * count * per_row + 4 :
    ]
    core_even = place[0] == 0
    early = place[1] == 0
    width = na.shape[1]
    rows = na.shape[0] // count
    hidden = act.shape[1]
    targets = (nm, dhid, act, gy, na, dqkv, ctx, gmid)
    waits = []
    for index, target in enumerate(targets):
        for row in range(count):
            waits.append(
                fetch(
                    early,
                    sources[row * per_row + index],
                    sources[(count + row) * per_row + index],
                    target.at[pl.ds(row * rows, rows)],
                    sems.at[index * count + row],
                )
            )
    for wait in waits[: 2 * count]:
        wait.wait()
    nm_t[...] = nm[...].T

    def up_step(tile, carry):
        cols = columns(tile, TILE)
        grad_up[:, cols] = dot_nn(nm_t[...], dhid[:, cols]).astype(BF16)
        return carry

    lax.fori_loop(0, hidden // TILE, up_step, 0)
    base = 8 * count
    put_up = deliver(core_even, grad_up, other_first, own_first, sems.at[base])
    for wait in waits[2 * count : 4 * count]:
        wait.wait()
    half = hidden // 2

    def down_low(tile, carry):
        cols = columns(tile, GROUP)
        grad_low[cols, :] = dot_nn(act[:, cols].T, gy[...]).astype(BF16)
        return carry

    def down_high(tile, carry):
        cols = pl.ds(pl.multiple_of(half + tile * GROUP, GROUP), GROUP)
        grad_high[columns(tile, GROUP), :] = dot_nn(act[:, cols].T, gy[...]).astype(BF16)
        return carry

    lax.fori_loop(0, half // GROUP, down_low, 0)
    put_low = deliver(core_even, grad_low, own_half, other_half, sems.at[base + 1])
    lax.fori_loop(0, half // GROUP, down_high, 0)
    put_high = deliver(core_even, grad_high, other_half, own_half, sems.at[base + 2])
    for wait in waits[4 * count :]:
        wait.wait()
    na_t[...] = na[...].T
    ctx_t[...] = ctx[...].T

    def in_step(tile, carry):
        cols = columns(tile, width)
        grad_att[:, cols] = dot_nn(na_t[...], dqkv[:, cols]).astype(BF16)
        return carry

    lax.fori_loop(0, 3, in_step, 0)
    grad_att[:, 3 * width :] = dot_nn(ctx_t[...], gmid[...]).astype(BF16)
    put_att = deliver(core_even, grad_att, own_first, other_first, sems.at[base + 3])
    for put in (put_up, put_low, put_high, put_att):
        put.wait()


def weight_call(place, early_rows, late_rows):
    count = len(early_rows)
    rows, width = early_rows[0][0].shape
    hidden = early_rows[0][1].shape[1]
    flat = [array for row in (*early_rows, *late_rows) for array in row]
    low = lambda *shape: jax.ShapeDtypeStruct(shape, BF16)
    outs = [low(width, hidden), low(hidden // 2, width), low(width, hidden), low(hidden // 2, width)]
    v = pltpu.VMEM
    all_rows = count * rows
    return pl.pallas_call(
        partial(weight_kernel, count),
        out_shape=outs,
        in_specs=[SMEM] + [ANY] * len(flat),
        out_specs=[ANY] * 4,
        scratch_shapes=[
            v((all_rows, width), BF16), v((all_rows, width), BF16), v((all_rows, 3 * width), BF16),
            v((all_rows, hidden), BF16), v((all_rows, width), BF16), v((all_rows, hidden), BF16),
            v((all_rows, width), BF16), v((all_rows, width), BF16),
            v((width, all_rows), BF16), v((width, all_rows), BF16), v((width, all_rows), BF16),
            v((width, hidden), BF16), v((width, hidden), BF16), v((hidden // 2, width), BF16), v((hidden // 2, width), BF16),
            pltpu.SemaphoreType.DMA((8 * count + 4,)),
        ],
        compiler_params=pltpu.CompilerParams(vmem_limit_bytes=VMEM_LIMIT),
        cost_estimate=pl.CostEstimate(flops=10_000_000_000, bytes_accessed=30_000_000, transcendentals=0),
        name="weight_gradients",
    )(place, *flat)


def ring_reduce(pieces, extras, axis):
    members = lax.axis_size(axis)
    order = list(range(0, members, 2)) + list(range(members - 1, 0, -2))
    place_of = np.zeros(members, np.int32)
    for position, member in enumerate(order):
        place_of[member] = position
    ahead = [(order[i], order[(i + 1) % members]) for i in range(members)]
    behind = [(b, a) for a, b in ahead]
    position = jnp.asarray(place_of)[lax.axis_index(axis)]

    rings = [(piece, extra, way) for piece, extra in zip(pieces, extras) for way in (0, 1)]

    def chunk(ring, index):
        piece, extra, way = ring
        spot = lax.rem(index + 2 * members, members)
        mine = lax.dynamic_index_in_dim(piece[way], spot, 0, keepdims=False)
        return mine.astype(F32) + lax.dynamic_index_in_dim(extra[way], spot, 0, keepdims=False).astype(F32)

    steps = [1 if ring[2] == 0 else -1 for ring in rings]
    current = [chunk(ring, position).astype(BF16) for ring in rings]
    for number in range(1, members):
        for index, ring in enumerate(rings):
            moved = lax.ppermute(current[index], axis, ahead if ring[2] == 0 else behind)
            current[index] = (moved.astype(F32) + chunk(ring, position - steps[index] * number)).astype(BF16)
    gathered = []
    for index, ring in enumerate(rings):
        blank = jnp.zeros(ring[0].shape[1:], F32)
        gathered.append(
            lax.dynamic_update_index_in_dim(
                blank, current[index].astype(F32), lax.rem(position + steps[index] + 2 * members, members), 0
            )
        )
    for number in range(1, members):
        for index, ring in enumerate(rings):
            current[index] = lax.ppermute(current[index], axis, ahead if ring[2] == 0 else behind)
            spot = lax.rem(position + steps[index] * (1 - number) + 2 * members, members)
            gathered[index] = lax.dynamic_update_index_in_dim(gathered[index], current[index].astype(F32), spot, 0)
    return [jnp.stack(gathered[2 * i : 2 * i + 2]) for i in range(len(pieces))]


def shards(
    patches, cotangent, mask_flags, segments, mask_token, norm_gains, norm_shifts, w_first, first_bias, down_half
):
    section = lax.axis_index("section")
    core = lax.rem(section, 2)
    stage = section // 2
    early = stage == 0
    swap = [(0, 1), (1, 0), (2, 3), (3, 2)]
    forth = [(0, 2), (1, 3)]
    back = [(2, 0), (3, 1)]
    row_count, rows, width = patches.shape
    hidden = w_first.shape[2]
    count = row_count // 2

    first_own, half_own = w_first[0], down_half[0]
    vec_own = jnp.concatenate([norm_gains, norm_shifts, first_bias.reshape(hidden // width, width)], 0)
    vec_other = lax.ppermute(vec_own, "section", swap)
    first_other = lax.ppermute(first_own, "section", swap)
    half_other = lax.ppermute(half_own, "section", swap)
    weights = (first_own, first_other, half_own, half_other)
    vec_att = jnp.where(core == 0, vec_own, vec_other).astype(F32)
    vec_mlp = jnp.where(core == 0, vec_other, vec_own).astype(F32)
    bias_wide = vec_mlp[2:6].reshape(1, hidden)
    vec_mlp = jnp.concatenate([jnp.pad(vec_mlp, ((0, 0), (0, hidden - width))), bias_wide], 0)

    def mine(array):
        return lax.dynamic_slice_in_dim(array, core * count, count, 0)

    my_flags = mine(mask_flags)
    starts = jnp.where(my_flags[..., None] == 1, mask_token, mine(patches))
    my_segments = mine(segments)
    my_cotangent = mine(cotangent)
    place = jnp.stack([core, stage]).astype(jnp.int32)

    def clamp(value):
        return min(max(value, 0), count - 1)

    forwards = []
    sent = starts[0]
    for slot in range(count + 1):
        seg = jnp.where(early, my_segments[clamp(slot)], my_segments[clamp(slot - 1)])
        result = forward_call(
            place, starts[clamp(slot)], sent, vec_att, vec_mlp, seg[None, :], seg[:, None], weights
        )
        forwards.append(result)
        if slot < count:
            sent = lax.ppermute(result[2], "section", forth)

    backs = []
    returned = my_cotangent[0]
    for slot in range(count + 1):
        flags = jnp.where(early, my_flags[clamp(slot - 1)], my_flags[clamp(slot)])
        active = jnp.where(early, slot >= 1, slot < count).astype(jnp.int32)
        saved = [
            [forwards[which][i] for i in (3, 4, 5, 6, 7, 9)] for which in (max(slot - 1, 0), min(slot + 1, count))
        ]
        result = backward_call(
            jnp.concatenate([place, active[None]]), my_cotangent[clamp(slot)], returned, vec_att, vec_mlp,
            flags[:, None], weights, *saved
        )
        backs.append(result)
        if slot < count:
            returned = lax.ppermute(result[2], "section", back)

    def gather_row(forward, backward):
        return (backward[5], backward[7], forward[8], backward[9], backward[4], backward[6], forward[7], backward[8])

    own_first, own_half, to_first, to_half = weight_call(
        place,
        [gather_row(forwards[row], backs[row + 1]) for row in range(count)],
        [gather_row(forwards[row + 1], backs[row]) for row in range(count)],
    )
    from_first = lax.ppermute(to_first, "section", swap)
    from_half = lax.ppermute(to_half, "section", swap)

    members = lax.axis_size("dp")
    first_shape = (2, members, width // (2 * members), hidden)
    half_shape = (2, members, half_own.shape[0] // (2 * members), width)
    grad_first, grad_half = ring_reduce(
        [own_first.reshape(first_shape), own_half.reshape(half_shape)],
        [from_first.reshape(first_shape), from_half.reshape(half_shape)],
        "dp",
    )

    small = sum(jnp.where(early, backs[row + 1][3], backs[row][3]) for row in range(count))
    small = jnp.concatenate([small[:8, :width], small[13].reshape(hidden // width, width), small[12:13, :width]], 0)
    small = jnp.where((jnp.arange(2) == stage)[:, None, None], small[None], 0.0)
    small = lax.psum(small, ("section", "dp"))
    token_grad = small[0, 12]
    here = lax.dynamic_index_in_dim(small, stage, 0, keepdims=False)
    here = lax.dynamic_slice_in_dim(here, 6 * core, 6, 0)

    def assemble(keep, send):
        received = lax.ppermute(send, "section", swap)
        return jnp.where(
            core == 0, jnp.concatenate([keep, received], 0), jnp.concatenate([received, keep], 0)
        )

    keep = jnp.stack([jnp.where(early, forwards[row][0], forwards[row + 1][0]) for row in range(count)])
    send = jnp.stack([jnp.where(early, forwards[row][1], forwards[row + 1][1]) for row in range(count)])
    finals = assemble(keep, send)
    keep = jnp.stack([jnp.where(early, backs[row + 1][0], backs[row][0]) for row in range(count)])
    send = jnp.stack([jnp.where(early, backs[row + 1][1], backs[row][1]) for row in range(count)])
    back_rows = assemble(keep, send).astype(F32)
    back_rows = jnp.where((section == 0) & (mask_flags[..., None] == 1), 0.0, back_rows)
    return (
        finals[None],
        back_rows[None],
        token_grad,
        here[0:1],
        here[1:2],
        grad_first.reshape(1, width, hidden),
        here[2:6].reshape(1, hidden),
        grad_half.reshape(1, half_own.shape[0], width),
    )


def solution(mesh):
    return jax.shard_map(
        shards,
        mesh=mesh,
        in_specs=(
            P("dp", None, None),
            P("dp", None, None),
            P("dp", None),
            P("dp", None),
            P(),
            P("section", None),
            P("section", None),
            P("section", None, None),
            P("section", None),
            P("section", None, None),
        ),
        out_specs=(
            P("section", "dp", None, None),
            P("section", "dp", None, None),
            P(),
            P("section", None),
            P("section", None),
            P("section", None, None),
            P("section", None),
            P("section", None, None),
        ),
        check_vma=False,
    )
```

time: 1390 us -> 592 us (0.43)
  other arithmetic: 355 us -> 32.1 us
  matrix products: 195 us -> 0 us
  local copies, waits for them, and re-layouts: 171 us -> 28 us
  Pallas kernels: 0 us -> 138 us
  blocking collectives: 109 us -> 0 us
  waiting for transfers between devices: 398 us -> 293 us
  starting transfers between devices: 97.1 us -> 68.2 us
  loops' own time: 28.3 us -> 0 us
    psum x1, waiting for transfers between devices: 353 us -> 116 us  [shards(): small = lax.psum(small, ('section', 'dp'))]
    add x36 -> x1, other arithmetic: 180 us -> 0.97 us  [shards(): sum((jnp.where(early, backs[row + 1][3], backs[row][3]) for row in range(...]
    dot_general x52 -> x0, matrix products: 156 us -> none  [the longest x12 39.1 us: product(): return jnp.dot(matrix_a, matrix_b, preferred_element_type=jnp.float32)]
    pallas_call x0 -> x7, Pallas kernels: none -> 138 us  [the longest x3 62.1 us: forward_call(): pl.pallas_call(forward_kernel, out_shape=outs, in_specs=[SMEM, ANY, ANY,...]
    ppermute x18 -> x67, waiting for transfers between devices: 44.6 us -> 177 us  [the longest x56 134 us: ring_reduce(): lax.ppermute(current[index], axis, ahead if ring[2] == 0 else behind)]
    psum x2 -> x0, blocking collectives: 109 us -> none  [the longest x1 69.2 us: shards(): token_grad = lax.psum(token_total, ('section', 'dp'))]
    scatter x21 -> x0, other arithmetic: 57.2 us -> none  [the longest x7 21.7 us: backward_step(): back_rows.at[slot_index]]
    another operation x39 -> x5, local copies, waits for them, and re-layouts: 54.9 us -> 1.49 us  [the longest x4 1.48 us: ring_reduce(): return [jnp.stack(gathered[2 * i:2 * i + 2]) for i in range(len(pieces))]]
  transfers between devices with their start and end apart: 19 -> 68, of which waited for: 6 -> 49; matrix products, arithmetic and copies ran while one was open for 19% -> 8% of each run, Pallas kernels for 0% -> 12%
where the time goes in v1:
time: 592 us; the launch traced here: 584 us
  waiting for transfers between devices  293 us (49%)
  Pallas kernels  138 us (23%)
  starting transfers between devices  68.2 us (12%)
  other arithmetic  32.1 us (5%)
  local copies, waits for them, and re-layouts  28 us (5%)
  between operations  25.3 us (4%)
    ppermute x56, waiting for transfers between devices, ring_reduce(): lax.ppermute(current[index], axis, ahead if ring[2] == 0 else behind)  134 us
    psum x1, waiting for transfers between devices, shards(): small = lax.psum(small, ('section', 'dp'))  116 us
    pallas_call x3, Pallas kernels, forward_call(): pl.pallas_call(forward_kernel, out_shape=outs, in_specs=[SMEM, ANY, ANY,...  62.1 us
    ppermute x56, starting transfers between devices, ring_reduce(): lax.ppermute(current[index], axis, ahead if ring[2] == 0 else behind)  55.1 us
    pallas_call x3, Pallas kernels, backward_call(): pl.pallas_call(backward_kernel, out_shape=outs, in_specs=[SMEM, ANY, ANY,...  53.1 us
    ppermute x2, waiting for transfers between devices, shards(): returned = lax.ppermute(result[2], 'section', back)  24.1 us
    pallas_call x1, Pallas kernels, weight_call(): pl.pallas_call(partial(weight_kernel, count), out_shape=outs, in_specs=[S...  22.4 us
    ppermute x2, waiting for transfers between devices, shards(): sent = lax.ppermute(result[2], 'section', forth)  18.3 us
  transfers between devices with their start and end apart: 68, of which 49 were waited for; matrix products, arithmetic and copies ran while one was open for 8% of the time, Pallas kernels for 12%

profile of v1, /device:TPU:0, one launch (start us, length us, event | category | flops | bytes accessed | tf_op | source)
XLA Modules:
  0.0 583.7 jit_solution(11032604933087237710)
XLA Ops:
  17.1 2.3 dynamic-slice_bitcast_fusion
  33.4 20.7 %row_forward.3 = (bf16[352,768]{1,0:T(8,128)(2,1)}, bf16[352,768]{1,0:T(8,128)(2,1)}, bf16[352,768]{1,0:T(8,128)(2,1)}, bf16[352,768]{1,0:T(8,128)(2,1)}, bf16[3...) custom-call(s32[2]{0:T(128)} %pad_add_fusion.place, ...), custom_call_target="tpu_custom_call" | custom-call | flops 7000000000 | bytes 26000000 | tf_op jit(solution)/shard_map/row_forward/pallas_call | solution.py:195
  54.1 4.5 collective-permute-start.3
  60.6 10.4 %collective-permute-done.3.sent_row = bf16[352,768]{1,0:T(8,128)(2,1)S(1)} collective-permute-done((bf16[352,768]{1,0:T(8,128)(2,1)}, bf16[352,768]{1,0:T(8,128)(2,1)S(1)}, u32[]{:S(2)}, u32[]{:S(2)}) %collective-permute-start.3) | collective-permute-done | bytes 540704 | tf_op jit(solution)/shard_map/ppermute | solution.py:559
  71.8 20.7 %row_forward.4 = (bf16[352,768]{1,0:T(8,128)(2,1)}, bf16[352,768]{1,0:T(8,128)(2,1)}, bf16[352,768]{1,0:T(8,128)(2,1)}, bf16[352,768]{1,0:T(8,128)(2,1)}, bf16[3...) custom-call(s32[2]{0:T(128)} %pad_add_fusion.place, ...), custom_call_target="tpu_custom_call" | custom-call | flops 7000000000 | bytes 26000000 | tf_op jit(solution)/shard_map/row_forward/pallas_call | solution.py:195
  92.5 4.3 collective-permute-start.4
  96.8 2.4 row_backward.3
  100.5 7.9 %collective-permute-done.4.sent_row = bf16[352,768]{1,0:T(8,128)(2,1)S(1)} collective-permute-done((bf16[352,768]{1,0:T(8,128)(2,1)}, bf16[352,768]{1,0:T(8,128)(2,1)S(1)}, u32[]{:S(2)}, u32[]{:S(2)}) %collective-permute-start.4) | collective-permute-done | bytes 540704 | tf_op jit(solution)/shard_map/ppermute | solution.py:559
  109.2 20.7 %row_forward.5 = (bf16[352,768]{1,0:T(8,128)(2,1)}, bf16[352,768]{1,0:T(8,128)(2,1)}, bf16[352,768]{1,0:T(8,128)(2,1)}, bf16[352,768]{1,0:T(8,128)(2,1)}, bf16[3...) custom-call(s32[2]{0:T(128)} %pad_add_fusion.place, ...), custom_call_target="tpu_custom_call" | custom-call | flops 7000000000 | bytes 26000000 | tf_op jit(solution)/shard_map/row_forward/pallas_call | solution.py:195
  129.9 5.5 collective-permute-done.6.back_row
  136.2 25.4 %row_backward.4 = (bf16[352,768]{1,0:T(8,128)(2,1)}, bf16[352,768]{1,0:T(8,128)(2,1)}, bf16[352,768]{1,0:T(8,128)(2,1)}, f32[16,3072]{1,0:T(8,128)}, bf16[352,76...) custom-call(s32[3]{0:T(128)} %pad_add_fusion.1.place, ...), custom_call_target="tpu_custom_call" | custom-call | flops 8000000000 | bytes 34000000 | tf_op jit(solution)/shard_map/row_backward/pallas_call | solution.py:354
  165.7 18.7 %collective-permute-done.7.back_row = bf16[352,768]{1,0:T(8,128)(2,1)S(1)} collective-permute-done((bf16[352,768]{1,0:T(8,128)(2,1)}, bf16[352,768]{1,0:T(8,128)(2,1)S(1)}, u32[]{:S(2)}, u32[]{:S(2)}) %collective-permute-start.7) | collective-permute-done | bytes 540704 | tf_op jit(solution)/shard_map/ppermute | solution.py:575
  185.2 25.3 %row_backward.5 = (bf16[352,768]{1,0:T(8,128)(2,1)}, bf16[352,768]{1,0:T(8,128)(2,1)}, bf16[352,768]{1,0:T(8,128)(2,1)}, f32[16,3072]{1,0:T(8,128)}, bf16[352,76...) custom-call(s32[3]{0:T(128)} %pad_add_fusion.4.place, ...), custom_call_target="tpu_custom_call" | custom-call | flops 8000000000 | bytes 34000000 | tf_op jit(solution)/shard_map/row_backward/pallas_call | solution.py:354
  211.6 22.4 %weight_gradients.1 = (bf16[768,3072]{1,0:T(8,128)(2,1)}, bf16[1536,768]{1,0:T(8,128)(2,1)}, bf16[768,3072]{1,0:T(8,128)(2,1)}, bf16[1536,768]{1,0:T(8,128)(2,1)}) custom-call(s32[2]{0:T(128)} %pad_add_fusion.place, bf16[352,768]{1,0:T(8,128)(2,1)} %get-tuple-element.107.refs_0_.refs_24_, bf16[352,3072]{1,0:T(8,128)(2,1)} %get-tuple-element.108.refs_1_.refs_25_, ...), custom_call_target="tpu_custom_call" | custom-call | flops 10000000000 | bytes 30000000 | tf_op jit(solution)/shard_map/weight_gradients/pallas_call | solution.py:454
  236.6 4.4 fusion.42
  243.8 116.0 %all-reduce.3.cloned.1.call-done = f32[2,13,768]{2,1,0:T(8,128)} async-done(((f32[2,13,768]{2,1,0:T(8,128)}), f32[2,13,768]{2,1,0:T(8,128)}) %all-reduce.3.cloned.1.call-update) | async-done | bytes 79888 | tf_op jit(solution)/shard_map/psum | solution.py:600
  366.8 2.8 maximum_select_fusion
  373.1 3.4 collective-permute-done.39
  379.3 4.3 collective-permute-done.40
  385.9 3.7 collective-permute-done.41
  391.8 3.0 collective-permute-done.42
  397.1 3.3 collective-permute-done.43
  402.7 4.3 collective-permute-done.44
  409.5 3.6 collective-permute-done.45
  414.0 3.7 convert_select_fusion
  419.7 4.5 collective-permute-done.61
  426.3 3.9 collective-permute-done.62
  432.3 3.1 collective-permute-done.63
  437.6 3.1 collective-permute-done.64
  442.7 4.5 collective-permute-done.65
  449.4 3.8 collective-permute-done.66
  455.3 2.6 pad_maximum_fusion.1
  457.9 2.8 fusion.43
  463.2 7.0 %collective-permute-done.24 = bf16[48,3072]{1,0:T(8,128)(2,1)S(1)} collective-permute-done((bf16[48,3072]{1,0:T(8,128)(2,1)S(1)}, bf16[48,3072]{1,0:T(8,128)(2,1)S(1)}, u32[]{:S(2)}, u32[]{:S(2)}) %collective-permute-start.24) | collective-permute-done | bytes 294944 | tf_op jit(solution)/shard_map/ppermute | solution.py:495
  472.8 6.0 %collective-permute-done.25 = bf16[48,3072]{1,0:T(8,128)(2,1)S(1)} collective-permute-done((bf16[48,3072]{1,0:T(8,128)(2,1)S(1)}, bf16[48,3072]{1,0:T(8,128)(2,1)S(1)}, u32[]{:S(2)}, u32[]{:S(2)}) %collective-permute-start.25) | collective-permute-done | bytes 294944 | tf_op jit(solution)/shard_map/ppermute | solution.py:495
  481.2 5.8 collective-permute-done.26
  489.4 4.9 collective-permute-done.27
  496.7 5.1 collective-permute-done.28
  504.2 6.5 %collective-permute-done.29 = bf16[48,3072]{1,0:T(8,128)(2,1)S(1)} collective-permute-done((bf16[48,3072]{1,0:T(8,128)(2,1)S(1)}, bf16[48,3072]{1,0:T(8,128)(2,1)S(1)}, u32[]{:S(2)}, u32[]{:S(2)}) %collective-permute-start.29) | collective-permute-done | bytes 294944 | tf_op jit(solution)/shard_map/ppermute | solution.py:495
  513.1 7.6 %collective-permute-done.30 = bf16[48,3072]{1,0:T(8,128)(2,1)S(1)} collective-permute-done((bf16[48,3072]{1,0:T(8,128)(2,1)S(1)}, bf16[48,3072]{1,0:T(8,128)(2,1)S(1)}, u32[]{:S(2)}, u32[]{:S(2)}) %collective-permute-start.30) | collective-permute-done | bytes 294944 | tf_op jit(solution)/shard_map/ppermute | solution.py:495
  524.2 5.5 collective-permute-done.31
  532.0 5.0 collective-permute-done.32
  539.2 4.5 collective-permute-done.33
  545.9 4.5 collective-permute-done.34
  552.6 4.5 collective-permute-done.35
  559.3 4.5 collective-permute-done.36
  566.0 4.5 collective-permute-done.37
  572.1 4.4 pad_maximum_fusion
  (284 shorter events, 106.2 us)
Async XLA Ops:
  7.2 352.6 %all-reduce.3.cloned.1.call-start = ((), (), s32[]{:S(2)}) async-start(), calls=%async_computation | async-start | bytes 196608 | tf_op jit(solution)/shard_map/psum | solution.py:600
  7.2 24.7 %collective-permute-start.1 = (bf16[768,3072]{1,0:T(8,128)(2,1)}, bf16[768,3072]{1,0:T(8,128)(2,1)}, u32[]{:S(2)}, u32[]{:S(2)}) collective-permute-start(bf16[768,3072]{1,0:T(8,128)(2,1)} %bitcast.294), channel_id=1, source_target_pairs={{0,8},{8,0},{16,24},{24,16},{1,9},{9,1},{17,25},{25,17},{2,10},{10... | collective-permute-start | bytes 14155784 | tf_op jit(solution)/shard_map/ppermute | solution.py:530
  9.2 21.3 %collective-permute-start = (bf16[6,768]{1,0:T(8,128)(2,1)S(1)}, bf16[6,768]{1,0:T(8,128)(2,1)S(1)}, u32[]{:S(2)}, u32[]{:S(2)}) collective-permute-start(bf16[6,768]{1,0:T(8,128)(2,1)S(1)} %pad_maximum_fusion.5), channel_id=1, source_target_pairs={{0,8},{8,0},{16,24},{24,16},{1,9},{9,1},{17,25},{25,17},{2,10},{10... | collective-permute-start | bytes 27656 | tf_op jit(solution)/shard_map/ppermute | solution.py:529
  9.4 22.5 %collective-permute-start.2 = (bf16[1536,768]{1,0:T(8,128)(2,1)}, bf16[1536,768]{1,0:T(8,128)(2,1)S(1)}, u32[]{:S(2)}, u32[]{:S(2)}) collective-permute-start(bf16[1536,768]{1,0:T(8,128)(2,1)} %bitcast.301), channel_id=1, source_target_pairs={{0,8},{8,0},{16,24},{24,16},{1,9},{9,1},{17,25},{25,17},{2,10},{10... | collective-permute-start | bytes 7077896 | tf_op jit(solution)/shard_map/ppermute | solution.py:531
  54.1 16.9 %collective-permute-start.3 = (bf16[352,768]{1,0:T(8,128)(2,1)}, bf16[352,768]{1,0:T(8,128)(2,1)S(1)}, u32[]{:S(2)}, u32[]{:S(2)}) collective-permute-start(bf16[352,768]{1,0:T(8,128)(2,1)} %get-tuple-element.71), channel_id=1, source_target_pairs={{0,16},{8,24},{1,17},{9,25},{2,18},{10,26},{3,19},{11,27},{4,20},{... | collective-permute-start | bytes 1622024 | tf_op jit(solution)/shard_map/ppermute | solution.py:559
  92.5 15.9 %collective-permute-start.4 = (bf16[352,768]{1,0:T(8,128)(2,1)}, bf16[352,768]{1,0:T(8,128)(2,1)S(1)}, u32[]{:S(2)}, u32[]{:S(2)}) collective-permute-start(bf16[352,768]{1,0:T(8,128)(2,1)} %get-tuple-element.73), channel_id=1, source_target_pairs={{0,16},{8,24},{1,17},{9,25},{2,18},{10,26},{3,19},{11,27},{4,20},{... | collective-permute-start | bytes 1622024 | tf_op jit(solution)/shard_map/ppermute | solution.py:559
  99.2 36.1 %collective-permute-start.6 = (bf16[352,768]{1,0:T(8,128)(2,1)}, bf16[352,768]{1,0:T(8,128)(2,1)S(1)}, u32[]{:S(2)}, u32[]{:S(2)}) collective-permute-start(bf16[352,768]{1,0:T(8,128)(2,1)} %get-tuple-element.90), channel_id=1, source_target_pairs={{16,0},{24,8},{17,1},{25,9},{18,2},{26,10},{19,3},{27,11},{20,4},{... | collective-permute-start | bytes 1622024 | tf_op jit(solution)/shard_map/ppermute | solution.py:575
  161.6 22.8 %collective-permute-start.7 = (bf16[352,768]{1,0:T(8,128)(2,1)}, bf16[352,768]{1,0:T(8,128)(2,1)S(1)}, u32[]{:S(2)}, u32[]{:S(2)}) collective-permute-start(bf16[352,768]{1,0:T(8,128)(2,1)} %get-tuple-element.99), channel_id=1, source_target_pairs={{16,0},{24,8},{17,1},{25,9},{18,2},{26,10},{19,3},{27,11},{20,4},{... | collective-permute-start | bytes 1622024 | tf_op jit(solution)/shard_map/ppermute | solution.py:575
  164.1 202.7 %collective-permute-start.5 = (bf16[2,352,768]{2,1,0:T(8,128)(2,1)}, bf16[2,352,768]{2,1,0:T(8,128)(2,1)}, u32[]{:S(2)}, u32[]{:S(2)}) collective-permute-start(bf16[2,352,768]{2,1,0:T(8,128)(2,1)} %pad_maximum_fusion.2), channel_id=1, source_target_pairs={{0,8},{8,0},{16,24},{24,16},{1,9},{9,1},{17,25},{25,17},{2,10},{10... | collective-permute-start | bytes 3244040 | tf_op jit(solution)/shard_map/ppermute | solution.py:606
  233.9 129.3 %collective-permute-start.38 = (bf16[1536,768]{1,0:T(8,128)(2,1)}, bf16[1536,768]{1,0:T(8,128)(2,1)}, u32[]{:S(2)}, u32[]{:S(2)}) collective-permute-start(bf16[1536,768]{1,0:T(8,128)(2,1)} %get-tuple-element.131), channel_id=1, source_target_pairs={{0,8},{8,0},{16,24},{24,16},{1,9},{9,1},{17,25},{25,17},{2,10},{10... | collective-permute-start | bytes 7077896 | tf_op jit(solution)/shard_map/ppermute | solution.py:586
  235.2 178.7 %collective-permute-start.8 = (bf16[2,352,768]{2,1,0:T(8,128)(2,1)}, bf16[2,352,768]{2,1,0:T(8,128)(2,1)}, u32[]{:S(2)}, u32[]{:S(2)}) collective-permute-start(bf16[2,352,768]{2,1,0:T(8,128)(2,1)} %pad_maximum_fusion.3), channel_id=1, source_target_pairs={{0,8},{8,0},{16,24},{24,16},{1,9},{9,1},{17,25},{25,17},{2,10},{10... | collective-permute-start | bytes 3244040 | tf_op jit(solution)/shard_map/ppermute | solution.py:606
  236.5 221.4 %collective-permute-start.9 = (bf16[768,3072]{1,0:T(8,128)(2,1)}, bf16[768,3072]{1,0:T(8,128)(2,1)}, u32[]{:S(2)}, u32[]{:S(2)}) collective-permute-start(bf16[768,3072]{1,0:T(8,128)(2,1)} %get-tuple-element.129), channel_id=1, source_target_pairs={{0,8},{8,0},{16,24},{24,16},{1,9},{9,1},{17,25},{25,17},{2,10},{10... | collective-permute-start | bytes 14155784 | tf_op jit(solution)/shard_map/ppermute | solution.py:585
  369.7 6.8 %collective-permute-start.39 = (bf16[96,768]{1,0:T(8,128)(2,1)S(1)}, bf16[96,768]{1,0:T(8,128)(2,1)S(1)}, u32[]{:S(2)}, u32[]{:S(2)}) collective-permute-start(bf16[96,768]{1,0:T(8,128)(2,1)S(1)} %fusion.30), channel_id=1, source_target_pairs={{0,2},{2,4},{4,6},{6,7},{7,5},{5,3},{3,1},{1,0},{8,10},{10,12},{12... | collective-permute-start | bytes 442376 | tf_op jit(solution)/shard_map/ppermute | solution.py:495
  376.6 7.1 %collective-permute-start.40 = (bf16[96,768]{1,0:T(8,128)(2,1)S(1)}, bf16[96,768]{1,0:T(8,128)(2,1)S(1)}, u32[]{:S(2)}, u32[]{:S(2)}) collective-permute-start(bf16[96,768]{1,0:T(8,128)(2,1)S(1)} %fusion.29), channel_id=1, source_target_pairs={{0,2},{2,4},{4,6},{6,7},{7,5},{5,3},{3,1},{1,0},{8,10},{10,12},{12... | collective-permute-start | bytes 442376 | tf_op jit(solution)/shard_map/ppermute | solution.py:495
  377.6 6.9 %collective-permute-start.55 = (bf16[96,768]{1,0:T(8,128)(2,1)S(1)}, bf16[96,768]{1,0:T(8,128)(2,1)S(1)}, u32[]{:S(2)}, u32[]{:S(2)}) collective-permute-start(bf16[96,768]{1,0:T(8,128)(2,1)S(1)} %fusion.21), channel_id=1, source_target_pairs={{2,0},{4,2},{6,4},{7,6},{5,7},{3,5},{1,3},{0,1},{10,8},{12,10},{14... | collective-permute-start | bytes 442376 | tf_op jit(solution)/shard_map/ppermute | solution.py:495
  400.5 6.5 %collective-permute-start.44 = (bf16[96,768]{1,0:T(8,128)(2,1)S(1)}, bf16[96,768]{1,0:T(8,128)(2,1)S(1)}, u32[]{:S(2)}, u32[]{:S(2)}) collective-permute-start(bf16[96,768]{1,0:T(8,128)(2,1)S(1)} %fusion.25), channel_id=1, source_target_pairs={{0,2},{2,4},{4,6},{6,7},{7,5},{5,3},{3,1},{1,0},{8,10},{10,12},{12... | collective-permute-start | bytes 442376 | tf_op jit(solution)/shard_map/ppermute | solution.py:495
  407.4 10.2 %collective-permute-start.60 = (bf16[96,768]{1,0:T(8,128)(2,1)S(1)}, bf16[96,768]{1,0:T(8,128)(2,1)S(1)}, u32[]{:S(2)}, u32[]{:S(2)}) collective-permute-start(bf16[96,768]{1,0:T(8,128)(2,1)S(1)} %get-tuple-element.135), channel_id=1, source_target_pairs={{2,0},{4,2},{6,4},{7,6},{5,7},{3,5},{1,3},{0,1},{10,8},{12,10},{14... | collective-permute-start | bytes 442376 | tf_op jit(solution)/shard_map/ppermute | solution.py:507
  417.6 6.6 %collective-permute-start.61 = (bf16[96,768]{1,0:T(8,128)(2,1)S(1)}, bf16[96,768]{1,0:T(8,128)(2,1)S(1)}, u32[]{:S(2)}, u32[]{:S(2)}) collective-permute-start(bf16[96,768]{1,0:T(8,128)(2,1)S(1)} %collective-permute-done.60), channel_id=1, source_target_pairs={{2,0},{4,2},{6,4},{7,6},{5,7},{3,5},{1,3},{0,1},{10,8},{12,10},{14... | collective-permute-start | bytes 442376 | tf_op jit(solution)/shard_map/ppermute | solution.py:507
  440.6 6.6 %collective-permute-start.65 = (bf16[96,768]{1,0:T(8,128)(2,1)S(1)}, bf16[96,768]{1,0:T(8,128)(2,1)S(1)}, u32[]{:S(2)}, u32[]{:S(2)}) collective-permute-start(bf16[96,768]{1,0:T(8,128)(2,1)S(1)} %collective-permute-done.64), channel_id=1, source_target_pairs={{2,0},{4,2},{6,4},{7,6},{5,7},{3,5},{1,3},{0,1},{10,8},{12,10},{14... | collective-permute-start | bytes 442376 | tf_op jit(solution)/shard_map/ppermute | solution.py:507
  442.2 6.7 %collective-permute-start.51 = (bf16[96,768]{1,0:T(8,128)(2,1)S(1)}, bf16[96,768]{1,0:T(8,128)(2,1)S(1)}, u32[]{:S(2)}, u32[]{:S(2)}) collective-permute-start(bf16[96,768]{1,0:T(8,128)(2,1)S(1)} %collective-permute-done.50), channel_id=1, source_target_pairs={{0,2},{2,4},{4,6},{6,7},{7,5},{5,3},{3,1},{1,0},{8,10},{10,12},{12... | collective-permute-start | bytes 442376 | tf_op jit(solution)/shard_map/ppermute | solution.py:507
  461.0 9.2 %collective-permute-start.24 = (bf16[48,3072]{1,0:T(8,128)(2,1)S(1)}, bf16[48,3072]{1,0:T(8,128)(2,1)S(1)}, u32[]{:S(2)}, u32[]{:S(2)}) collective-permute-start(bf16[48,3072]{1,0:T(8,128)(2,1)S(1)} %fusion.15), channel_id=1, source_target_pairs={{2,0},{4,2},{6,4},{7,6},{5,7},{3,5},{1,3},{0,1},{10,8},{12,10},{14... | collective-permute-start | bytes 884744 | tf_op jit(solution)/shard_map/ppermute | solution.py:495
  462.5 9.7 %collective-permute-start.10 = (bf16[48,3072]{1,0:T(8,128)(2,1)S(1)}, bf16[48,3072]{1,0:T(8,128)(2,1)S(1)}, u32[]{:S(2)}, u32[]{:S(2)}) collective-permute-start(bf16[48,3072]{1,0:T(8,128)(2,1)S(1)} %fusion.14), channel_id=1, source_target_pairs={{0,2},{2,4},{4,6},{6,7},{7,5},{5,3},{3,1},{1,0},{8,10},{10,12},{12... | collective-permute-start | bytes 884744 | tf_op jit(solution)/shard_map/ppermute | solution.py:495
  470.3 8.5 %collective-permute-start.25 = (bf16[48,3072]{1,0:T(8,128)(2,1)S(1)}, bf16[48,3072]{1,0:T(8,128)(2,1)S(1)}, u32[]{:S(2)}, u32[]{:S(2)}) collective-permute-start(bf16[48,3072]{1,0:T(8,128)(2,1)S(1)} %fusion.6), channel_id=1, source_target_pairs={{2,0},{4,2},{6,4},{7,6},{5,7},{3,5},{1,3},{0,1},{10,8},{12,10},{14... | collective-permute-start | bytes 884744 | tf_op jit(solution)/shard_map/ppermute | solution.py:495
  472.4 8.4 %collective-permute-start.11 = (bf16[48,3072]{1,0:T(8,128)(2,1)S(1)}, bf16[48,3072]{1,0:T(8,128)(2,1)S(1)}, u32[]{:S(2)}, u32[]{:S(2)}) collective-permute-start(bf16[48,3072]{1,0:T(8,128)(2,1)S(1)} %fusion.13), channel_id=1, source_target_pairs={{0,2},{2,4},{4,6},{6,7},{7,5},{5,3},{3,1},{1,0},{8,10},{10,12},{12... | collective-permute-start | bytes 884744 | tf_op jit(solution)/shard_map/ppermute | solution.py:495
  478.9 8.1 %collective-permute-start.26 = (bf16[48,3072]{1,0:T(8,128)(2,1)S(1)}, bf16[48,3072]{1,0:T(8,128)(2,1)S(1)}, u32[]{:S(2)}, u32[]{:S(2)}) collective-permute-start(bf16[48,3072]{1,0:T(8,128)(2,1)S(1)} %fusion.5), channel_id=1, source_target_pairs={{2,0},{4,2},{6,4},{7,6},{5,7},{3,5},{1,3},{0,1},{10,8},{12,10},{14... | collective-permute-start | bytes 884744 | tf_op jit(solution)/shard_map/ppermute | solution.py:495
  480.8 8.1 %collective-permute-start.12 = (bf16[48,3072]{1,0:T(8,128)(2,1)S(1)}, bf16[48,3072]{1,0:T(8,128)(2,1)S(1)}, u32[]{:S(2)}, u32[]{:S(2)}) collective-permute-start(bf16[48,3072]{1,0:T(8,128)(2,1)S(1)} %fusion.12), channel_id=1, source_target_pairs={{0,2},{2,4},{4,6},{6,7},{7,5},{5,3},{3,1},{1,0},{8,10},{10,12},{12... | collective-permute-start | bytes 884744 | tf_op jit(solution)/shard_map/ppermute | solution.py:495
  487.1 7.1 %collective-permute-start.27 = (bf16[48,3072]{1,0:T(8,128)(2,1)S(1)}, bf16[48,3072]{1,0:T(8,128)(2,1)S(1)}, u32[]{:S(2)}, u32[]{:S(2)}) collective-permute-start(bf16[48,3072]{1,0:T(8,128)(2,1)S(1)} %fusion.4), channel_id=1, source_target_pairs={{2,0},{4,2},{6,4},{7,6},{5,7},{3,5},{1,3},{0,1},{10,8},{12,10},{14... | collective-permute-start | bytes 884744 | tf_op jit(solution)/shard_map/ppermute | solution.py:495
  489.1 7.3 %collective-permute-start.13 = (bf16[48,3072]{1,0:T(8,128)(2,1)S(1)}, bf16[48,3072]{1,0:T(8,128)(2,1)S(1)}, u32[]{:S(2)}, u32[]{:S(2)}) collective-permute-start(bf16[48,3072]{1,0:T(8,128)(2,1)S(1)} %fusion.11), channel_id=1, source_target_pairs={{0,2},{2,4},{4,6},{6,7},{7,5},{5,3},{3,1},{1,0},{8,10},{10,12},{12... | collective-permute-start | bytes 884744 | tf_op jit(solution)/shard_map/ppermute | solution.py:495
  494.4 7.5 %collective-permute-start.28 = (bf16[48,3072]{1,0:T(8,128)(2,1)S(1)}, bf16[48,3072]{1,0:T(8,128)(2,1)S(1)}, u32[]{:S(2)}, u32[]{:S(2)}) collective-permute-start(bf16[48,3072]{1,0:T(8,128)(2,1)S(1)} %fusion.3), channel_id=1, source_target_pairs={{2,0},{4,2},{6,4},{7,6},{5,7},{3,5},{1,3},{0,1},{10,8},{12,10},{14... | collective-permute-start | bytes 884744 | tf_op jit(solution)/shard_map/ppermute | solution.py:495
  496.5 7.4 %collective-permute-start.14 = (bf16[48,3072]{1,0:T(8,128)(2,1)S(1)}, bf16[48,3072]{1,0:T(8,128)(2,1)S(1)}, u32[]{:S(2)}, u32[]{:S(2)}) collective-permute-start(bf16[48,3072]{1,0:T(8,128)(2,1)S(1)} %fusion.10), channel_id=1, source_target_pairs={{0,2},{2,4},{4,6},{6,7},{7,5},{5,3},{3,1},{1,0},{8,10},{10,12},{12... | collective-permute-start | bytes 884744 | tf_op jit(solution)/shard_map/ppermute | solution.py:495
  501.9 8.7 %collective-permute-start.29 = (bf16[48,3072]{1,0:T(8,128)(2,1)S(1)}, bf16[48,3072]{1,0:T(8,128)(2,1)S(1)}, u32[]{:S(2)}, u32[]{:S(2)}) collective-permute-start(bf16[48,3072]{1,0:T(8,128)(2,1)S(1)} %fusion.2), channel_id=1, source_target_pairs={{2,0},{4,2},{6,4},{7,6},{5,7},{3,5},{1,3},{0,1},{10,8},{12,10},{14... | collective-permute-start | bytes 884744 | tf_op jit(solution)/shard_map/ppermute | solution.py:495
  504.0 7.6 %collective-permute-start.15 = (bf16[48,3072]{1,0:T(8,128)(2,1)S(1)}, bf16[48,3072]{1,0:T(8,128)(2,1)S(1)}, u32[]{:S(2)}, u32[]{:S(2)}) collective-permute-start(bf16[48,3072]{1,0:T(8,128)(2,1)S(1)} %fusion.9), channel_id=1, source_target_pairs={{0,2},{2,4},{4,6},{6,7},{7,5},{5,3},{3,1},{1,0},{8,10},{10,12},{12... | collective-permute-start | bytes 884744 | tf_op jit(solution)/shard_map/ppermute | solution.py:495
  510.8 9.9 %collective-permute-start.30 = (bf16[48,3072]{1,0:T(8,128)(2,1)S(1)}, bf16[48,3072]{1,0:T(8,128)(2,1)S(1)}, u32[]{:S(2)}, u32[]{:S(2)}) collective-permute-start(bf16[48,3072]{1,0:T(8,128)(2,1)S(1)} %fusion.1), channel_id=1, source_target_pairs={{2,0},{4,2},{6,4},{7,6},{5,7},{3,5},{1,3},{0,1},{10,8},{12,10},{14... | collective-permute-start | bytes 884744 | tf_op jit(solution)/shard_map/ppermute | solution.py:495
  511.8 9.8 %collective-permute-start.16 = (bf16[48,3072]{1,0:T(8,128)(2,1)S(1)}, bf16[48,3072]{1,0:T(8,128)(2,1)S(1)}, u32[]{:S(2)}, u32[]{:S(2)}) collective-permute-start(bf16[48,3072]{1,0:T(8,128)(2,1)S(1)} %fusion.8), channel_id=1, source_target_pairs={{0,2},{2,4},{4,6},{6,7},{7,5},{5,3},{3,1},{1,0},{8,10},{10,12},{12... | collective-permute-start | bytes 884744 | tf_op jit(solution)/shard_map/ppermute | solution.py:495
  521.4 8.3 %collective-permute-start.31 = (bf16[48,3072]{1,0:T(8,128)(2,1)S(1)}, bf16[48,3072]{1,0:T(8,128)(2,1)S(1)}, u32[]{:S(2)}, u32[]{:S(2)}) collective-permute-start(bf16[48,3072]{1,0:T(8,128)(2,1)S(1)} %get-tuple-element.139), channel_id=1, source_target_pairs={{2,0},{4,2},{6,4},{7,6},{5,7},{3,5},{1,3},{0,1},{10,8},{12,10},{14... | collective-permute-start | bytes 884744 | tf_op jit(solution)/shard_map/ppermute | solution.py:507
  522.3 8.6 %collective-permute-start.17 = (bf16[48,3072]{1,0:T(8,128)(2,1)S(1)}, bf16[48,3072]{1,0:T(8,128)(2,1)S(1)}, u32[]{:S(2)}, u32[]{:S(2)}) collective-permute-start(bf16[48,3072]{1,0:T(8,128)(2,1)S(1)} %get-tuple-element.137), channel_id=1, source_target_pairs={{0,2},{2,4},{4,6},{6,7},{7,5},{5,3},{3,1},{1,0},{8,10},{10,12},{12... | collective-permute-start | bytes 884744 | tf_op jit(solution)/shard_map/ppermute | solution.py:507
  529.7 7.3 %collective-permute-start.32 = (bf16[48,3072]{1,0:T(8,128)(2,1)S(1)}, bf16[48,3072]{1,0:T(8,128)(2,1)S(1)}, u32[]{:S(2)}, u32[]{:S(2)}) collective-permute-start(bf16[48,3072]{1,0:T(8,128)(2,1)S(1)} %collective-permute-done.31), channel_id=1, source_target_pairs={{2,0},{4,2},{6,4},{7,6},{5,7},{3,5},{1,3},{0,1},{10,8},{12,10},{14... | collective-permute-start | bytes 884744 | tf_op jit(solution)/shard_map/ppermute | solution.py:507
  530.9 7.5 %collective-permute-start.18 = (bf16[48,3072]{1,0:T(8,128)(2,1)S(1)}, bf16[48,3072]{1,0:T(8,128)(2,1)S(1)}, u32[]{:S(2)}, u32[]{:S(2)}) collective-permute-start(bf16[48,3072]{1,0:T(8,128)(2,1)S(1)} %collective-permute-done.17), channel_id=1, source_target_pairs={{0,2},{2,4},{4,6},{6,7},{7,5},{5,3},{3,1},{1,0},{8,10},{10,12},{12... | collective-permute-start | bytes 884744 | tf_op jit(solution)/shard_map/ppermute | solution.py:507
  537.0 6.7 %collective-permute-start.33 = (bf16[48,3072]{1,0:T(8,128)(2,1)S(1)}, bf16[48,3072]{1,0:T(8,128)(2,1)S(1)}, u32[]{:S(2)}, u32[]{:S(2)}) collective-permute-start(bf16[48,3072]{1,0:T(8,128)(2,1)S(1)} %collective-permute-done.32), channel_id=1, source_target_pairs={{2,0},{4,2},{6,4},{7,6},{5,7},{3,5},{1,3},{0,1},{10,8},{12,10},{14... | collective-permute-start | bytes 884744 | tf_op jit(solution)/shard_map/ppermute | solution.py:507
  538.4 6.7 %collective-permute-start.19 = (bf16[48,3072]{1,0:T(8,128)(2,1)S(1)}, bf16[48,3072]{1,0:T(8,128)(2,1)S(1)}, u32[]{:S(2)}, u32[]{:S(2)}) collective-permute-start(bf16[48,3072]{1,0:T(8,128)(2,1)S(1)} %collective-permute-done.18), channel_id=1, source_target_pairs={{0,2},{2,4},{4,6},{6,7},{7,5},{5,3},{3,1},{1,0},{8,10},{10,12},{12... | collective-permute-start | bytes 884744 | tf_op jit(solution)/shard_map/ppermute | solution.py:507
  543.7 6.7 %collective-permute-start.34 = (bf16[48,3072]{1,0:T(8,128)(2,1)S(1)}, bf16[48,3072]{1,0:T(8,128)(2,1)S(1)}, u32[]{:S(2)}, u32[]{:S(2)}) collective-permute-start(bf16[48,3072]{1,0:T(8,128)(2,1)S(1)} %collective-permute-done.33), channel_id=1, source_target_pairs={{2,0},{4,2},{6,4},{7,6},{5,7},{3,5},{1,3},{0,1},{10,8},{12,10},{14... | collective-permute-start | bytes 884744 | tf_op jit(solution)/shard_map/ppermute | solution.py:507
  545.1 6.7 %collective-permute-start.20 = (bf16[48,3072]{1,0:T(8,128)(2,1)S(1)}, bf16[48,3072]{1,0:T(8,128)(2,1)S(1)}, u32[]{:S(2)}, u32[]{:S(2)}) collective-permute-start(bf16[48,3072]{1,0:T(8,128)(2,1)S(1)} %collective-permute-done.19), channel_id=1, source_target_pairs={{0,2},{2,4},{4,6},{6,7},{7,5},{5,3},{3,1},{1,0},{8,10},{10,12},{12... | collective-permute-start | bytes 884744 | tf_op jit(solution)/shard_map/ppermute | solution.py:507
  550.4 6.7 %collective-permute-start.35 = (bf16[48,3072]{1,0:T(8,128)(2,1)S(1)}, bf16[48,3072]{1,0:T(8,128)(2,1)S(1)}, u32[]{:S(2)}, u32[]{:S(2)}) collective-permute-start(bf16[48,3072]{1,0:T(8,128)(2,1)S(1)} %collective-permute-done.34), channel_id=1, source_target_pairs={{2,0},{4,2},{6,4},{7,6},{5,7},{3,5},{1,3},{0,1},{10,8},{12,10},{14... | collective-permute-start | bytes 884744 | tf_op jit(solution)/shard_map/ppermute | solution.py:507
  551.8 6.7 %collective-permute-start.21 = (bf16[48,3072]{1,0:T(8,128)(2,1)S(1)}, bf16[48,3072]{1,0:T(8,128)(2,1)S(1)}, u32[]{:S(2)}, u32[]{:S(2)}) collective-permute-start(bf16[48,3072]{1,0:T(8,128)(2,1)S(1)} %collective-permute-done.20), channel_id=1, source_target_pairs={{0,2},{2,4},{4,6},{6,7},{7,5},{5,3},{3,1},{1,0},{8,10},{10,12},{12... | collective-permute-start | bytes 884744 | tf_op jit(solution)/shard_map/ppermute | solution.py:507
  557.1 6.7 %collective-permute-start.36 = (bf16[48,3072]{1,0:T(8,128)(2,1)S(1)}, bf16[48,3072]{1,0:T(8,128)(2,1)S(1)}, u32[]{:S(2)}, u32[]{:S(2)}) collective-permute-start(bf16[48,3072]{1,0:T(8,128)(2,1)S(1)} %collective-permute-done.35), channel_id=1, source_target_pairs={{2,0},{4,2},{6,4},{7,6},{5,7},{3,5},{1,3},{0,1},{10,8},{12,10},{14... | collective-permute-start | bytes 884744 | tf_op jit(solution)/shard_map/ppermute | solution.py:507
  558.6 6.7 %collective-permute-start.22 = (bf16[48,3072]{1,0:T(8,128)(2,1)S(1)}, bf16[48,3072]{1,0:T(8,128)(2,1)S(1)}, u32[]{:S(2)}, u32[]{:S(2)}) collective-permute-start(bf16[48,3072]{1,0:T(8,128)(2,1)S(1)} %collective-permute-done.21), channel_id=1, source_target_pairs={{0,2},{2,4},{4,6},{6,7},{7,5},{5,3},{3,1},{1,0},{8,10},{10,12},{12... | collective-permute-start | bytes 884744 | tf_op jit(solution)/shard_map/ppermute | solution.py:507
  563.9 6.7 %collective-permute-start.37 = (bf16[48,3072]{1,0:T(8,128)(2,1)S(1)}, bf16[48,3072]{1,0:T(8,128)(2,1)S(1)}, u32[]{:S(2)}, u32[]{:S(2)}) collective-permute-start(bf16[48,3072]{1,0:T(8,128)(2,1)S(1)} %collective-permute-done.36), channel_id=1, source_target_pairs={{2,0},{4,2},{6,4},{7,6},{5,7},{3,5},{1,3},{0,1},{10,8},{12,10},{14... | collective-permute-start | bytes 884744 | tf_op jit(solution)/shard_map/ppermute | solution.py:507
  565.3 6.7 %collective-permute-start.23 = (bf16[48,3072]{1,0:T(8,128)(2,1)S(1)}, bf16[48,3072]{1,0:T(8,128)(2,1)S(1)}, u32[]{:S(2)}, u32[]{:S(2)}) collective-permute-start(bf16[48,3072]{1,0:T(8,128)(2,1)S(1)} %collective-permute-done.22), channel_id=1, source_target_pairs={{0,2},{2,4},{4,6},{6,7},{7,5},{5,3},{3,1},{1,0},{8,10},{10,12},{12... | collective-permute-start | bytes 884744 | tf_op jit(solution)/shard_map/ppermute | solution.py:507
  (57 other events, 587.9 us)
Sparse Core Ops, SparseCore 0:
  236.6 123.1 all-reduce.2
